TPU v7x, 32 devices: a whole 2x2x4 slice. The times are simulated.
32 devices in a mesh: group: 2 (over x), gx: 8 (over z, y), gy: 2 (over core).
Axes of the slice: x: 2, y: 2, z: 4, core: 2. Of those that a mesh axis runs over, the one named last changes fastest.
Arguments:
- easting_current: float32 [16, 1024, 256], P(None, ('group', 'gx'), 'gy'), parts along dimension 1, may hold values from -3 to 3
- poleward_current: float32 [16, 1024, 256], P(None, ('group', 'gx'), 'gy'), parts along dimension 1, may hold values from -3 to 3
- thermal_anomaly: float32 [16, 1024, 256], P(None, ('group', 'gx'), 'gy'), parts along dimension 1, may hold values from -6 to 6
- planetary_spin_parameter: float32 [512], P('gx'), may hold values from -1 to 1
- stratum_spacings: float32 [16], replicated, may hold values from 0.5 to 2
- sideways_diffusivity: float32 [512, 256], P('gx', 'gy'), may hold values from 0.03 to 0.2
- bathymetry_multiplier: float32 [512, 256], P('gx', 'gy'), may hold values from 0.5 to 2
- sea_level_elevation: float32 [1024, 256], P(('group', 'gx'), 'gy'), parts along dimension 0, may hold values from -12 to 12
- wet_dry_indicator: int32 [8, 4], replicated, may hold values 0 or 1
Outputs:
- easting_current_next: float32 [16, 1024, 256], P(None, ('group', 'gx'), 'gy'), parts along dimension 1
- poleward_current_next: float32 [16, 1024, 256], P(None, ('group', 'gx'), 'gy'), parts along dimension 1
- thermal_anomaly_next: float32 [16, 1024, 256], P(None, ('group', 'gx'), 'gy'), parts along dimension 1
- barotropic_guess: float32 [1024, 256], P(('group', 'gx'), 'gy'), parts along dimension 0
- equation_misfit: float32 [1024, 256], P(('group', 'gx'), 'gy'), parts along dimension 0
There are 2 independent parts, one for each index of `group`. A program takes and returns all parts, laid end to end along the dimension named above; an argument that names none is the same for every part. Nothing has to cross between parts.
All inputs are finite; a program needn't handle non-finite values.
Results may differ from a plain program's by a relative error of at most 0.0003.
Values sent between devices are 32-bit elements; how exact they have to be, the bound alone decides.
A program may use at most 128 MiB of HBM per device.

v0:
```python
import jax
import jax.numpy as jnp
from jax import lax
from jax.sharding import PartitionSpec as P

TS = 64
ITERS = 3


pressure_coef = 0.02
biharmonic_coef = 0.02
advection_coef = 0.5
surface_coef = 0.5
divergence_coef = 0.1


def with_halo(cells, sides, width):
    for axis, dim in sides:
        count = lax.axis_size(axis)
        ends = count - 1
        head = lax.slice_in_dim(cells, 0, width, axis=dim)
        tail = lax.slice_in_dim(cells, cells.shape[dim] - width, cells.shape[dim], axis=dim)
        cells = jnp.concatenate(
            [
                lax.ppermute(tail, axis, [(i, (i + 1) % count) for i in range(ends)]),
                cells,
                lax.ppermute(head, axis, [((i + 1) % count, i) for i in range(ends)]),
            ],
            axis=dim,
        )
    return cells


def ocean_cells(wet_dry_indicator, row_start, column_start, row_count, column_count, margin):
    tile_rows = wet_dry_indicator.shape[0]
    tile_columns = wet_dry_indicator.shape[1]
    row_index = row_start - margin + jnp.arange(row_count + 2 * margin, dtype=jnp.int32)
    column_index = column_start - margin + jnp.arange(column_count + 2 * margin, dtype=jnp.int32)
    row_pick = (
        (row_index[:, None] // TS == jnp.arange(tile_rows, dtype=jnp.int32)[None, :])
        & (row_index[:, None] >= 0)
    ).astype(jnp.float32)
    column_pick = (
        (column_index[:, None] // TS == jnp.arange(tile_columns, dtype=jnp.int32)[None, :])
        & (column_index[:, None] >= 0)
    ).astype(jnp.float32)
    tiles = wet_dry_indicator.astype(jnp.float32)
    partial_rows = jnp.dot(row_pick, tiles, precision=lax.Precision.HIGHEST)
    return jnp.dot(partial_rows, column_pick.T, precision=lax.Precision.HIGHEST)


def faces(wet_cell_indicator, coefficient):
    row_faces = (
        0.5
        * (coefficient[1:, :] + coefficient[:-1, :])
        * wet_cell_indicator[1:, :]
        * wet_cell_indicator[:-1, :]
    )
    column_faces = (
        0.5
        * (coefficient[:, 1:] + coefficient[:, :-1])
        * wet_cell_indicator[:, 1:]
        * wet_cell_indicator[:, :-1]
    )
    return (row_faces, column_faces)


def diffuse(values, row_faces, column_faces):
    flux_row = row_faces * (values[..., 1:, :] - values[..., :-1, :])
    flux_column = column_faces * (values[..., :, 1:] - values[..., :, :-1])
    return (
        flux_row[..., 1:, 1:-1]
        - flux_row[..., :-1, 1:-1]
        + (flux_column[..., 1:-1, 1:] - flux_column[..., 1:-1, :-1])
    )


def stratified_advance(
    haloed_array, wet_cell_indicator, planetary_spin_parameter, stratum_spacings
):
    levels = stratum_spacings.shape[0]
    zonal = haloed_array[:levels]
    meridional = haloed_array[levels : 2 * levels]
    tracer = haloed_array[2 * levels : 3 * levels]
    viscosity = haloed_array[3 * levels]
    unit_rows, unit_columns = faces(wet_cell_indicator, jnp.ones_like(wet_cell_indicator))
    inner_rows = unit_rows[1:-1, 1:-1]
    inner_columns = unit_columns[1:-1, 1:-1]
    mask_inner = wet_cell_indicator[1:-1, 1:-1]
    visc_rows, visc_columns = faces(mask_inner, viscosity[1:-1, 1:-1])
    zonal_inner = zonal[:, 1:-1, 1:-1]
    meridional_inner = meridional[:, 1:-1, 1:-1]
    tracer_inner = tracer[:, 1:-1, 1:-1]
    thickness = stratum_spacings[:, None, None]
    column = tracer_inner * thickness
    geopotential = jnp.cumsum(column, axis=0) - 0.5 * column
    centre = geopotential[:, 1:-1, 1:-1]
    grad_row = 0.5 * (
        mask_inner[2:, 1:-1] * (geopotential[:, 2:, 1:-1] - centre)
        + mask_inner[:-2, 1:-1] * (centre - geopotential[:, :-2, 1:-1])
    )
    grad_column = 0.5 * (
        mask_inner[1:-1, 2:] * (geopotential[:, 1:-1, 2:] - centre)
        + mask_inner[1:-1, :-2] * (centre - geopotential[:, 1:-1, :-2])
    )
    flux_row = (
        0.25
        * (zonal_inner[:, 1:, :] + zonal_inner[:, :-1, :])
        * (tracer_inner[:, 1:, :] + tracer_inner[:, :-1, :])
        * inner_rows
    )
    flux_column = (
        0.25
        * (meridional_inner[:, :, 1:] + meridional_inner[:, :, :-1])
        * (tracer_inner[:, :, 1:] + tracer_inner[:, :, :-1])
        * inner_columns
    )
    spread = (
        flux_row[:, 1:, 1:-1]
        - flux_row[:, :-1, 1:-1]
        + (flux_column[:, 1:-1, 1:] - flux_column[:, 1:-1, :-1])
    )
    hyper_zonal = diffuse(diffuse(zonal, unit_rows, unit_columns), inner_rows, inner_columns)
    hyper_meridional = diffuse(
        diffuse(meridional, unit_rows, unit_columns), inner_rows, inner_columns
    )
    core_mask = wet_cell_indicator[2:-2, 2:-2]
    rotation = planetary_spin_parameter[:, None]
    zonal_core = zonal[:, 2:-2, 2:-2]
    meridional_core = meridional[:, 2:-2, 2:-2]
    tracer_core = tracer[:, 2:-2, 2:-2]
    easting_current_next = core_mask * (
        zonal_core
        + rotation * meridional_core
        - pressure_coef * grad_row
        + diffuse(zonal_inner, visc_rows, visc_columns)
        - biharmonic_coef * hyper_zonal
    )
    poleward_current_next = core_mask * (
        meridional_core
        - rotation * zonal_core
        - pressure_coef * grad_column
        + diffuse(meridional_inner, visc_rows, visc_columns)
        - biharmonic_coef * hyper_meridional
    )
    tracer_next = core_mask * (
        tracer_core - advection_coef * spread + diffuse(tracer_inner, visc_rows, visc_columns)
    )
    return (easting_current_next, poleward_current_next, tracer_next)


def surface_setup(
    padded_zonal, padded_meridional, padded_depth, sea_level_elevation, wet_cell_indicator
):
    row_faces, column_faces = faces(wet_cell_indicator, padded_depth)
    core_mask = wet_cell_indicator[1:-1, 1:-1]
    diverge = 0.5 * (padded_zonal[2:, 1:-1] - padded_zonal[:-2, 1:-1]) + 0.5 * (
        padded_meridional[1:-1, 2:] - padded_meridional[1:-1, :-2]
    )
    right_side = core_mask * (surface_coef * sea_level_elevation - divergence_coef * diverge)
    scaling = (
        surface_coef
        + row_faces[1:, 1:-1]
        + row_faces[:-1, 1:-1]
        + column_faces[1:-1, 1:]
        + column_faces[1:-1, :-1]
    )
    return (row_faces, column_faces, right_side, scaling)


def operate(padded_values, row_faces, column_faces):
    return surface_coef * padded_values[1:-1, 1:-1] - diffuse(
        padded_values, row_faces, column_faces
    )


def conjugate(right_side, scaling, row_faces, column_faces, extend, norm_sum, curvature_sum):
    solution = jnp.zeros_like(right_side)
    residual = right_side
    scaled = residual / scaling
    direction = scaled
    residual_dot = norm_sum(residual * scaled)
    for iteration in range(ITERS):
        image = operate(extend(direction), row_faces, column_faces)
        step_size = residual_dot / curvature_sum(direction * image)
        solution = solution + step_size * direction
        residual = residual - step_size * image
        if iteration + 1 < ITERS:
            scaled = residual / scaling
            dot_next = norm_sum(residual * scaled)
            direction = scaled + dot_next / residual_dot * direction
            residual_dot = dot_next
    return (solution, residual)


def per_device(
    easting_current,
    poleward_current,
    thermal_anomaly,
    planetary_spin_parameter,
    stratum_spacings,
    sideways_diffusivity,
    bathymetry_multiplier,
    sea_level_elevation,
    wet_dry_indicator,
):
    row_count = easting_current.shape[1]
    column_count = easting_current.shape[2]
    row_start = lax.axis_index("gx") * row_count
    column_start = lax.axis_index("gy") * column_count
    wet_cell_indicator = ocean_cells(
        wet_dry_indicator, row_start, column_start, row_count, column_count, 2
    )
    bundled_arrays = jnp.concatenate(
        [easting_current, poleward_current, thermal_anomaly, sideways_diffusivity[None]], axis=0
    )
    haloed_array = with_halo(bundled_arrays, (("gx", 1), ("gy", 2)), 2)
    easting_current_next, poleward_current_next, thermal_anomaly_next = stratified_advance(
        haloed_array, wet_cell_indicator, planetary_spin_parameter, stratum_spacings
    )
    thickness = stratum_spacings[:, None, None]
    transport_u = jnp.sum(easting_current_next * thickness, axis=0)
    transport_v = jnp.sum(poleward_current_next * thickness, axis=0)
    rim_fields = with_halo(
        jnp.stack([transport_u, transport_v, bathymetry_multiplier]), (("gx", 1), ("gy", 2)), 1
    )
    row_faces, column_faces, right_side, scaling = surface_setup(
        rim_fields[0],
        rim_fields[1],
        rim_fields[2],
        sea_level_elevation,
        wet_cell_indicator[1:-1, 1:-1],
    )

    def extend(values):
        return with_halo(values, (("gx", 0), ("gy", 1)), 1)

    def norm_sum(values):
        return lax.psum(jnp.sum(values), ("gx", "gy"))

    def curvature_sum(values):
        return lax.psum(jnp.sum(values), ("gx", "gy"))

    barotropic_guess, equation_misfit = conjugate(
        right_side, scaling, row_faces, column_faces, extend, norm_sum, curvature_sum
    )
    return (
        easting_current_next,
        poleward_current_next,
        thermal_anomaly_next,
        barotropic_guess,
        equation_misfit,
    )


def solution(mesh):
    placed = (
        P(None, ("group", "gx"), "gy"),
        P(None, ("group", "gx"), "gy"),
        P(None, ("group", "gx"), "gy"),
        P("gx"),
        P(),
        P("gx", "gy"),
        P("gx", "gy"),
        P(("group", "gx"), "gy"),
        P(),
    )
    return jax.shard_map(
        per_device,
        mesh=mesh,
        in_specs=placed,
        out_specs=(
            P(None, ("group", "gx"), "gy"),
            P(None, ("group", "gx"), "gy"),
            P(None, ("group", "gx"), "gy"),
            P(("group", "gx"), "gy"),
            P(("group", "gx"), "gy"),
        ),
        check_vma=False,
    )
```

profile of v0, /device:TPU:0, one launch (start us, length us, event | category | flops | bytes accessed | tf_op | source)
XLA Modules:
  0.0 333.2 jit_solution(11879217776199795243)
XLA Ops:
  0.6 0.9 copy.34
  1.6 1.4 copy.37
  3.3 1.8 copy.33
  6.1 3.9 %fusion.89 = (f32[49,2,128]{1,2,0:T(8,128)}, f32[49,2,128]{1,2,0:T(8,128)}) fusion(f32[49,64,128]{1,2,0:T(8,128)S(1)} %pad_maximum_fusion.1), kind=kLoop, calls=%fused_computation.214 | loop fusion | bytes 200704 | tf_op jit(solution)/shard_map/slice | solution.py:22
  9.9 2.7 copy.39
  12.7 1.3 collective-permute-start.1
  14.0 2.0 copy.38
  16.0 6.1 %collective-permute-start = (f32[49,2,128]{2,1,0:T(2,128)}, f32[49,2,128]{2,1,0:T(2,128)}, u32[]{:S(2)}, u32[]{:S(2)}) collective-permute-start(f32[49,2,128]{2,1,0:T(2,128)} %copy.38), channel_id=1, source_target_pairs={{0,2},{2,4},{4,6},{6,8},{8,10},{10,12},{12,14},{1,3},{3,5},{5,7},{... | collective-permute-start | bytes 150536 | tf_op jit(solution)/shard_map/ppermute | solution.py:25
  22.6 0.9 fusion.91
  23.5 1.6 copy.41
  25.2 3.0 copy.40
  28.1 2.1 pad_maximum_fusion.26
  30.2 1.3 collective-permute-start.3
  31.5 3.6 %collective-permute-start.2 = (f32[49,68,2]{1,2,0:T(2,128)}, f32[49,68,2]{1,2,0:T(2,128)}, u32[]{:S(2)}, u32[]{:S(2)}) collective-permute-start(f32[49,68,2]{1,2,0:T(2,128)} %get-tuple-element.42), channel_id=1, source_target_pairs={{0,1},{2,3},{4,5},{6,7},{8,9},{10,11},{12,13},{14,15},{16,17},{18,... | collective-permute-start | bytes 79976 | tf_op jit(solution)/shard_map/ppermute | solution.py:25
  36.7 1.5 copy.48
  38.8 5.7 %pad_maximum_fusion = f32[49,68,132]{1,2,0:T(8,128)S(1)} fusion(f32[49,68,2]{1,2,0:T(2,128)} %copy-done.37, f32[49,2,128]{1,2,0:T(8,128)} %copy-done, f32[1,64,128]{1,2,0:T(8,128)S(1)} %bitcast.22, f32[16,64,128]{1,2,0:T(8,128)} %copy-done.3, f32[16,64,128]{1,2,0:T(8,128)} %copy-done.5, f32[16,64,128]{1,2,0:T(8,128)} %copy-done.7, f32[49,2,128]{1,2,0:T(8,128)} %copy.40, ...), kind=kLoop, calls=%fused_computation | loop fusion | flops 3078768 | bytes 3518592 | tf_op jit(solution)/shard_map/concatenate | solution.py:23
  46.1 0.8 fusion.52
  47.0 1.8 fusion.2
  48.8 1.6 fusion.6
  50.5 2.0 fusion.7
  52.5 3.9 %subtract_multiply_fusion.1 = (f32[16,65,130]{1,2,0:T(8,128)}, f32[16,65,130]{1,2,0:T(8,128)}, f32[16,65,130]{1,2,0:T(8,128)}, f32[16,65,130]{1,2,0:T(8,128)}) fusion(f32[49,68,132]{1,2,0:T(8,128)S(1)} %pad_maximum_fusion, f32[65,130]{0,1:T(8,128)S(1)} %fusion.55, f32[65,130]{0,1:T(8,128)S(1)} %copy-done.29), kind=kLoop, calls=%fused_computation.44 | loop fusion | flops 1487200 | bytes 5475600 | tf_op jit(solution)/shard_map/mul | solution.py:69
  56.4 1.5 slice_multiply_fusion
  57.9 2.9 copy.42
  60.8 2.5 fusion.95
  63.3 2.8 copy.43
  66.1 1.8 multiply_subtract_fusion
  68.4 13.1 %multiply_multiply_fusion = (f32[16,66,129]{1,2,0:T(8,128)}, f32[16,66,129]{1,2,0:T(8,128)}, f32[16,66,129]{1,2,0:T(8,128)}, f32[16,66,129]{1,2,0:T(8,128)}, f32[16,66,129]{1,2,0:T(8,128)}) fusion(f32[66,129]{0,1:T(8,128)S(1)} %copy-done.24, f32[49,2,128]{1,2,0:T(8,128)S(1)} %copy-done.1, f32[1,64,128]{1,2,0:T(8,128)S(1)} %bitcast.23, ...), kind=kLoop, calls=%fused_computation.45 | loop fusion | flops 3950496 | bytes 4517832 | tf_op jit(solution)/shard_map/mul | solution.py:113
  81.6 5.4 %subtract_multiply_fusion = (f32[16,66,129]{1,2,0:T(8,128)}, f32[16,66,129]{1,2,0:T(8,128)S(1)}, f32[16,66,129]{1,2,0:T(8,128)S(1)}) fusion(f32[16,66,129]{1,2,0:T(8,128)} %get-tuple-element.39, f32[16,66,129]{1,2,0:T(8,128)} %get-tuple-element.38, f32[66,129]{0,1:T(8,128)S(1)} %copy-done.39, f32[16,66,129]{1,2,0:T(8,128)} %get-tuple-element.41, ...), kind=kLoop, calls=%fused_computation.43 | loop fusion | flops 2452032 | bytes 5607624 | tf_op jit(solution)/shard_map/mul | solution.py:70
  87.1 7.2 %multiply_reduce_fusion.1 = (f32[64,128]{0,1:T(8,128)S(1)}, f32[64,128]{0,1:T(8,128)S(1)}, f32[16,64,128]{1,2,0:T(8,128)}, f32[16,64,128]{1,2,0:T(8,128)}) fusion(f32[16]{0:T(128)S(1)} %copy-done.46, f32[16,66,129]{1,2,0:T(8,128)S(1)} %copy-done.15, f32[16,65,130]{1,2,0:T(8,128)} %get-tuple-element.76, f32[16,66,129]{1,2,0:T(8,128)S(1)} %get-tuple-element.68, ...), kind=kLoop, calls=%fused_computation.95 | loop fusion | flops 5488640 | bytes 13336896 | tf_op jit(solution)/shard_map/reduce_sum | solution.py:222
  94.4 1.3 collective-permute-start.5
  95.7 4.9 %collective-permute-start.4 = (f32[3,1,128]{1,2,0:T(8,128)S(1)}, f32[3,1,128]{1,2,0:T(8,128)S(1)}, u32[]{:S(2)}, u32[]{:S(2)}) collective-permute-start(f32[3,1,128]{1,2,0:T(8,128)S(1)} %get-tuple-element.65), channel_id=1, source_target_pairs={{0,2},{2,4},{4,6},{6,8},{8,10},{10,12},{12,14},{1,3},{3,5},{5,7},{... | collective-permute-start | bytes 4616 | tf_op jit(solution)/shard_map/ppermute | solution.py:25
  100.6 2.1 collective-permute-done.5
  102.7 4.4 %collective-permute-done.4 = f32[3,1,128]{1,2,0:T(8,128)S(1)} collective-permute-done((f32[3,1,128]{1,2,0:T(8,128)S(1)}, f32[3,1,128]{1,2,0:T(8,128)S(1)}, u32[]{:S(2)}, u32[]{:S(2)}) %collective-permute-start.4) | collective-permute-done | bytes 1568 | tf_op jit(solution)/shard_map/ppermute | solution.py:25
  107.1 1.3 collective-permute-start.7
  108.4 3.0 collective-permute-start.6
  113.0 1.3 collective-permute-start.9
  114.3 5.0 %collective-permute-start.8 = (f32[1,128]{0,1:T(8,128)S(1)}, f32[1,128]{0,1:T(8,128)S(1)}, u32[]{:S(2)}, u32[]{:S(2)}) collective-permute-start(f32[1,128]{0,1:T(8,128)S(1)} %get-tuple-element.83), channel_id=1, source_target_pairs={{0,2},{2,4},{4,6},{6,8},{8,10},{10,12},{12,14},{1,3},{3,5},{5,7},{... | collective-permute-start | bytes 1544 | tf_op jit(solution)/shard_map/ppermute | solution.py:25
  119.9 1.6 collective-permute-done.8
  121.6 1.3 collective-permute-start.11
  122.9 3.0 collective-permute-start.10
  125.9 0.8 collective-permute-done.10
  127.1 0.7 multiply_reduce_fusion.6
  127.8 35.3 %all-reduce = (f32[]{:T(128)}, f32[]{:T(128)}) all-reduce(f32[]{:T(128)} %get-tuple-element.16, f32[]{:T(128)} %get-tuple-element.15), channel_id=1, replica_groups=mesh['group'=2,'gx'=8,'gy'=2] {'gx','gy'}, use_global_device_ids=true, to_apply=%region_4.5 | all-reduce | flops 2 | bytes 16 | tf_op jit(solution)/shard_map/psum | solution.py:239
  164.4 1.2 multiply_reduce_fusion.5
  165.7 30.1 %psum.44 = f32[]{:T(128)} all-reduce(f32[]{:T(128)} %get-tuple-element.28), channel_id=1, replica_groups=mesh['group'=2,'gx'=8,'gy'=2] {'gx','gy'}, use_global_device_ids=true, to_apply=%region_8.9 | all-reduce | flops 1 | bytes 8 | tf_op jit(solution)/shard_map/psum | solution.py:239
  197.2 1.3 collective-permute-start.13
  198.6 4.7 %collective-permute-start.12 = (f32[1,128]{0,1:T(8,128)S(1)}, f32[1,128]{0,1:T(8,128)S(1)}, u32[]{:S(2)}, u32[]{:S(2)}) collective-permute-start(f32[1,128]{0,1:T(8,128)S(1)} %get-tuple-element.81), channel_id=1, source_target_pairs={{0,2},{2,4},{4,6},{6,8},{8,10},{10,12},{12,14},{1,3},{3,5},{5,7},{... | collective-permute-start | bytes 1544 | tf_op jit(solution)/shard_map/ppermute | solution.py:25
  203.4 1.7 collective-permute-done.12
  205.2 1.3 collective-permute-start.15
  206.5 3.0 collective-permute-start.14
  209.5 0.8 collective-permute-done.14
  211.4 30.4 %psum.45 = f32[]{:T(128)} all-reduce(f32[]{:T(128)} %get-tuple-element.26), channel_id=1, replica_groups=mesh['group'=2,'gx'=8,'gy'=2] {'gx','gy'}, use_global_device_ids=true, to_apply=%region_10.11 | all-reduce | flops 1 | bytes 8 | tf_op jit(solution)/shard_map/psum | solution.py:242
  243.2 2.1 multiply_reduce_fusion.3
  245.3 30.1 %psum.46 = f32[]{:T(128)} all-reduce(f32[]{:T(128)} %get-tuple-element.23), channel_id=1, replica_groups=mesh['group'=2,'gx'=8,'gy'=2] {'gx','gy'}, use_global_device_ids=true, to_apply=%region_12.13 | all-reduce | flops 1 | bytes 8 | tf_op jit(solution)/shard_map/psum | solution.py:239
  276.7 0.9 multiply_add_fusion.1
  277.7 1.3 collective-permute-start.17
  279.0 4.8 %collective-permute-start.16 = (f32[1,128]{0,1:T(8,128)S(1)}, f32[1,128]{0,1:T(8,128)S(1)}, u32[]{:S(2)}, u32[]{:S(2)}) collective-permute-start(f32[1,128]{0,1:T(8,128)S(1)} %get-tuple-element.79), channel_id=1, source_target_pairs={{0,2},{2,4},{4,6},{6,8},{8,10},{10,12},{12,14},{1,3},{3,5},{5,7},{... | collective-permute-start | bytes 1544 | tf_op jit(solution)/shard_map/ppermute | solution.py:25
  283.8 5.2 %fusion.14 = f32[16,64,128]{1,2,0:T(8,128)} fusion(f32[16,66,129]{1,2,0:T(8,128)} %get-tuple-element.67, f32[16,65,130]{1,2,0:T(8,128)S(1)} %copy-done.10, f32[16,64,128]{1,2,0:T(8,128)S(1)} %copy-done.4, f32[16,66,129]{1,2,0:T(8,128)} %get-tuple-element.37, f32[16,65,130]{1,2,0:T(8,128)S(1)} %copy-done.11, f32[64,128]{0,1:T(8,128)} %get-tuple-element.74), kind=kLoop, calls=%fused_computation.53 | loop fusion | flops 1310720 | bytes 5275648 | tf_op jit(solution)/shard_map/mul | solution.py:146
  290.2 1.3 collective-permute-start.19
  291.5 3.0 collective-permute-start.18
  294.6 2.3 copy.49
  296.9 1.1 copy.50
  298.1 1.1 copy.51
  300.4 30.1 %psum.47 = f32[]{:T(128)} all-reduce(f32[]{:T(128)} %get-tuple-element.21), channel_id=1, replica_groups=mesh['group'=2,'gx'=8,'gy'=2] {'gx','gy'}, use_global_device_ids=true, to_apply=%region_14.15 | all-reduce | flops 1 | bytes 8 | tf_op jit(solution)/shard_map/psum | solution.py:242
  (159 shorter events, 14.3 us)
Async XLA Ops:
  0.6 2.3 copy-start.36
  3.0 2.1 copy-start.3
  3.3 2.0 copy-start.5
  9.9 4.0 %copy-start.9 = (f32[49,2,128]{1,2,0:T(8,128)S(1)}, f32[49,2,128]{1,2,0:T(8,128)}, u32[]{:S(2)}) copy-start(f32[49,2,128]{1,2,0:T(8,128)} %get-tuple-element.52) | copy-start | bytes 150532
  12.7 10.9 %collective-permute-start.1 = (f32[49,2,128]{2,1,0:T(2,128)S(1)}, f32[49,2,128]{2,1,0:T(2,128)S(1)}, u32[]{:S(2)}, u32[]{:S(2)}) collective-permute-start(f32[49,2,128]{2,1,0:T(2,128)S(1)} %copy.39), channel_id=1, source_target_pairs={{2,0},{4,2},{6,4},{8,6},{10,8},{12,10},{14,12},{3,1},{5,3},{7,5},{... | collective-permute-start | bytes 150536 | tf_op jit(solution)/shard_map/ppermute | solution.py:27
  14.0 8.1 %copy-start.48 = (s32[8,4]{0,1:T(4,128)S(1)}, s32[8,4]{0,1:T(4,128)}, u32[]{:S(2)}) copy-start(s32[8,4]{0,1:T(4,128)} %param.17) | copy-start | bytes 388
  16.0 9.2 %collective-permute-start = (f32[49,2,128]{2,1,0:T(2,128)}, f32[49,2,128]{2,1,0:T(2,128)}, u32[]{:S(2)}, u32[]{:S(2)}) collective-permute-start(f32[49,2,128]{2,1,0:T(2,128)} %copy.38), channel_id=1, source_target_pairs={{0,2},{2,4},{4,6},{6,8},{8,10},{10,12},{12,14},{1,3},{3,5},{5,7},{... | collective-permute-start | bytes 150536 | tf_op jit(solution)/shard_map/ppermute | solution.py:25
  23.5 11.8 %copy-start.25 = (f32[68,131]{0,1:T(8,128)}, f32[68,131]{0,1:T(8,128)S(1)}, u32[]{:S(2)}) copy-start(f32[68,131]{0,1:T(8,128)S(1)} %slice_multiply_fusion.1) | copy-start | bytes 106900
  25.1 3.0 copy-start
  30.2 8.0 %collective-permute-start.3 = (f32[49,68,2]{1,2,0:T(2,128)}, f32[49,68,2]{1,2,0:T(2,128)S(1)}, u32[]{:S(2)}, u32[]{:S(2)}) collective-permute-start(f32[49,68,2]{1,2,0:T(2,128)} %get-tuple-element.43), channel_id=1, source_target_pairs={{1,0},{3,2},{5,4},{7,6},{9,8},{11,10},{13,12},{15,14},{17,16},{19,... | collective-permute-start | bytes 79976 | tf_op jit(solution)/shard_map/ppermute | solution.py:27
  31.5 7.3 %collective-permute-start.2 = (f32[49,68,2]{1,2,0:T(2,128)}, f32[49,68,2]{1,2,0:T(2,128)}, u32[]{:S(2)}, u32[]{:S(2)}) collective-permute-start(f32[49,68,2]{1,2,0:T(2,128)} %get-tuple-element.42), channel_id=1, source_target_pairs={{0,1},{2,3},{4,5},{6,7},{8,9},{10,11},{12,13},{14,15},{16,17},{18,... | collective-permute-start | bytes 79976 | tf_op jit(solution)/shard_map/ppermute | solution.py:25
  35.3 2.9 copy-start.27
  38.2 6.3 %copy-start.26 = (f32[68,131]{0,1:T(8,128)S(1)}, f32[68,131]{0,1:T(8,128)}, u32[]{:S(2)}) copy-start(f32[68,131]{0,1:T(8,128)} %copy-done.25) | copy-start | bytes 106900
  47.0 1.8 copy-start.23
  48.8 1.6 copy-start.29
  52.5 3.9 %copy-start.46 = (f32[16]{0:T(128)S(1)}, f32[16]{0:T(128)}, u32[]{:S(2)}) copy-start(f32[16]{0:T(128)} %param.13) | copy-start | bytes 196
  66.1 2.2 copy-start.1
  66.1 2.2 copy-start.24
  66.1 2.2 copy-start.38
  68.3 13.1 %copy-start.2 = (f32[49,2,128]{1,2,0:T(8,128)S(1)}, f32[49,2,128]{1,2,0:T(8,128)}, u32[]{:S(2)}) copy-start(f32[49,2,128]{1,2,0:T(8,128)} %copy.40) | copy-start | bytes 150532
  68.3 13.1 %copy-start.4 = (f32[16,64,128]{1,2,0:T(8,128)S(1)}, f32[16,64,128]{1,2,0:T(8,128)}, u32[]{:S(2)}) copy-start(f32[16,64,128]{1,2,0:T(8,128)} %copy-done.3) | copy-start | bytes 1572868
  68.3 13.1 %copy-start.6 = (f32[16,64,128]{1,2,0:T(8,128)S(1)}, f32[16,64,128]{1,2,0:T(8,128)}, u32[]{:S(2)}) copy-start(f32[16,64,128]{1,2,0:T(8,128)} %copy-done.5) | copy-start | bytes 1572868
  68.3 13.1 %copy-start.8 = (f32[16,64,128]{1,2,0:T(8,128)S(1)}, f32[16,64,128]{1,2,0:T(8,128)}, u32[]{:S(2)}) copy-start(f32[16,64,128]{1,2,0:T(8,128)} %copy-done.7) | copy-start | bytes 1572868
  68.4 13.1 %copy-start.39 = (f32[66,129]{0,1:T(8,128)S(1)}, f32[66,129]{0,1:T(8,128)}, u32[]{:S(2)}) copy-start(f32[66,129]{0,1:T(8,128)} %fusion.52) | copy-start | bytes 102172
  81.5 5.5 %copy-start.12 = (f32[16,65,130]{1,2,0:T(8,128)S(1)}, f32[16,65,130]{1,2,0:T(8,128)}, u32[]{:S(2)}) copy-start(f32[16,65,130]{1,2,0:T(8,128)} %get-tuple-element.45) | copy-start | bytes 1622404
  81.5 5.5 %copy-start.13 = (f32[16,65,130]{1,2,0:T(8,128)S(1)}, f32[16,65,130]{1,2,0:T(8,128)}, u32[]{:S(2)}) copy-start(f32[16,65,130]{1,2,0:T(8,128)} %get-tuple-element.46) | copy-start | bytes 1622404
  81.5 5.5 %copy-start.14 = (f32[16,66,129]{1,2,0:T(8,128)S(1)}, f32[16,66,129]{1,2,0:T(8,128)}, u32[]{:S(2)}) copy-start(f32[16,66,129]{1,2,0:T(8,128)} %get-tuple-element.77) | copy-start | bytes 1634692
  81.5 5.5 %copy-start.15 = (f32[16,66,129]{1,2,0:T(8,128)S(1)}, f32[16,66,129]{1,2,0:T(8,128)}, u32[]{:S(2)}) copy-start(f32[16,66,129]{1,2,0:T(8,128)} %get-tuple-element.78) | copy-start | bytes 1634692
  81.5 5.5 %copy-start.16 = (f32[16,65,130]{1,2,0:T(8,128)S(1)}, f32[16,65,130]{1,2,0:T(8,128)}, u32[]{:S(2)}) copy-start(f32[16,65,130]{1,2,0:T(8,128)} %get-tuple-element.75) | copy-start | bytes 1622404
  81.5 5.5 %copy-start.35 = (f32[64,128]{0,1:T(8,128)S(1)}, f32[64,128]{0,1:T(8,128)}, u32[]{:S(2)}) copy-start(f32[64,128]{0,1:T(8,128)} %get-tuple-element.74) | copy-start | bytes 98308
  81.5 5.5 %copy-start.41 = (f32[64,128]{0,1:T(8,128)S(1)}, f32[64,128]{0,1:T(8,128)}, u32[]{:S(2)}) copy-start(f32[64,128]{0,1:T(8,128)} %get-tuple-element.70) | copy-start | bytes 98308
  81.5 5.5 %copy-start.42 = (f32[64,128]{0,1:T(8,128)S(1)}, f32[64,128]{0,1:T(8,128)}, u32[]{:S(2)}) copy-start(f32[64,128]{0,1:T(8,128)} %get-tuple-element.71) | copy-start | bytes 98308
  81.6 5.5 %copy-start.43 = (f32[64,128]{0,1:T(8,128)S(1)}, f32[64,128]{0,1:T(8,128)}, u32[]{:S(2)}) copy-start(f32[64,128]{0,1:T(8,128)} %get-tuple-element.72) | copy-start | bytes 98308
  81.6 5.5 %copy-start.44 = (f32[64,128]{0,1:T(8,128)S(1)}, f32[64,128]{0,1:T(8,128)}, u32[]{:S(2)}) copy-start(f32[64,128]{0,1:T(8,128)} %get-tuple-element.73) | copy-start | bytes 98308
  81.6 5.5 %copy-start.47 = (f32[64]{0:T(128)S(1)}, f32[64]{0:T(128)}, u32[]{:S(2)}) copy-start(f32[64]{0:T(128)} %param.12) | copy-start | bytes 772
  87.0 7.2 %copy-start.22 = (f32[64,128]{0,1:T(8,128)S(1)}, f32[64,128]{0,1:T(8,128)}, u32[]{:S(2)}) copy-start(f32[64,128]{0,1:T(8,128)} %copy.48) | copy-start | bytes 98308
  94.3 17.2 %copy-start.45 = (f32[64,128]{1,0:T(8,128)S(1)}, f32[64,128]{1,0:T(8,128)}, u32[]{:S(2)}) copy-start(f32[64,128]{1,0:T(8,128)} %param.16) | copy-start | bytes 98308
  94.4 8.3 %collective-permute-start.5 = (f32[3,1,128]{1,2,0:T(8,128)S(1)}, f32[3,1,128]{1,2,0:T(8,128)S(1)}, u32[]{:S(2)}, u32[]{:S(2)}) collective-permute-start(f32[3,1,128]{1,2,0:T(8,128)S(1)} %get-tuple-element.66), channel_id=1, source_target_pairs={{2,0},{4,2},{6,4},{8,6},{10,8},{12,10},{14,12},{3,1},{5,3},{7,5},{... | collective-permute-start | bytes 4616 | tf_op jit(solution)/shard_map/ppermute | solution.py:27
  95.7 11.3 %collective-permute-start.4 = (f32[3,1,128]{1,2,0:T(8,128)S(1)}, f32[3,1,128]{1,2,0:T(8,128)S(1)}, u32[]{:S(2)}, u32[]{:S(2)}) collective-permute-start(f32[3,1,128]{1,2,0:T(8,128)S(1)} %get-tuple-element.65), channel_id=1, source_target_pairs={{0,2},{2,4},{4,6},{6,8},{8,10},{10,12},{12,14},{1,3},{3,5},{5,7},{... | collective-permute-start | bytes 4616 | tf_op jit(solution)/shard_map/ppermute | solution.py:25
  107.1 4.4 %collective-permute-start.7 = (f32[3,66,1]{1,2,0:T(1,128)S(1)}, f32[3,66,1]{1,2,0:T(1,128)S(1)}, u32[]{:S(2)}, u32[]{:S(2)}) collective-permute-start(f32[3,66,1]{1,2,0:T(1,128)S(1)} %get-tuple-element.55), channel_id=1, source_target_pairs={{1,0},{3,2},{5,4},{7,6},{9,8},{11,10},{13,12},{15,14},{17,16},{19,... | collective-permute-start | bytes 2384 | tf_op jit(solution)/shard_map/ppermute | solution.py:27
  108.4 3.8 %collective-permute-start.6 = (f32[3,66,1]{1,2,0:T(1,128)S(1)}, f32[3,66,1]{1,2,0:T(1,128)S(1)}, u32[]{:S(2)}, u32[]{:S(2)}) collective-permute-start(f32[3,66,1]{1,2,0:T(1,128)S(1)} %get-tuple-element.54), channel_id=1, source_target_pairs={{0,1},{2,3},{4,5},{6,7},{8,9},{10,11},{12,13},{14,15},{16,17},{18,... | collective-permute-start | bytes 2384 | tf_op jit(solution)/shard_map/ppermute | solution.py:25
  112.6 14.5 %copy-start.19 = (f32[65,130]{0,1:T(8,128)}, f32[65,130]{0,1:T(8,128)S(1)}, u32[]{:S(2)}) copy-start(f32[65,130]{0,1:T(8,128)S(1)} %fusion.49) | copy-start | bytes 101404
  112.9 84.3 %copy-start.30 = (f32[64,128]{0,1:T(8,128)}, f32[64,128]{0,1:T(8,128)S(1)}, u32[]{:S(2)}) copy-start(f32[64,128]{0,1:T(8,128)S(1)} %get-tuple-element.33) | copy-start | bytes 98308
  113.0 7.0 %collective-permute-start.9 = (f32[1,128]{0,1:T(8,128)S(1)}, f32[1,128]{0,1:T(8,128)S(1)}, u32[]{:S(2)}, u32[]{:S(2)}) collective-permute-start(f32[1,128]{0,1:T(8,128)S(1)} %get-tuple-element.84), channel_id=1, source_target_pairs={{2,0},{4,2},{6,4},{8,6},{10,8},{12,10},{14,12},{3,1},{5,3},{7,5},{... | collective-permute-start | bytes 1544 | tf_op jit(solution)/shard_map/ppermute | solution.py:27
  114.3 7.2 %collective-permute-start.8 = (f32[1,128]{0,1:T(8,128)S(1)}, f32[1,128]{0,1:T(8,128)S(1)}, u32[]{:S(2)}, u32[]{:S(2)}) collective-permute-start(f32[1,128]{0,1:T(8,128)S(1)} %get-tuple-element.83), channel_id=1, source_target_pairs={{0,2},{2,4},{4,6},{6,8},{8,10},{10,12},{12,14},{1,3},{3,5},{5,7},{... | collective-permute-start | bytes 1544 | tf_op jit(solution)/shard_map/ppermute | solution.py:25
  121.6 4.3 %collective-permute-start.11 = (f32[66,1]{0,1:T(1,128)S(1)}, f32[66,1]{0,1:T(1,128)S(1)}, u32[]{:S(2)}, u32[]{:S(2)}) collective-permute-start(f32[66,1]{0,1:T(1,128)S(1)} %get-tuple-element.64), channel_id=1, source_target_pairs={{1,0},{3,2},{5,4},{7,6},{9,8},{11,10},{13,12},{15,14},{17,16},{19,... | collective-permute-start | bytes 800 | tf_op jit(solution)/shard_map/ppermute | solution.py:27
  122.9 3.8 %collective-permute-start.10 = (f32[66,1]{0,1:T(1,128)S(1)}, f32[66,1]{0,1:T(1,128)S(1)}, u32[]{:S(2)}, u32[]{:S(2)}) collective-permute-start(f32[66,1]{0,1:T(1,128)S(1)} %get-tuple-element.63), channel_id=1, source_target_pairs={{0,1},{2,3},{4,5},{6,7},{8,9},{10,11},{12,13},{14,15},{16,17},{18,... | collective-permute-start | bytes 800 | tf_op jit(solution)/shard_map/ppermute | solution.py:25
  127.1 83.4 %copy-start.20 = (f32[65,130]{0,1:T(8,128)S(1)}, f32[65,130]{0,1:T(8,128)}, u32[]{:S(2)}) copy-start(f32[65,130]{0,1:T(8,128)} %copy-done.19) | copy-start | bytes 101404
  197.2 6.2 %collective-permute-start.13 = (f32[1,128]{0,1:T(8,128)S(1)}, f32[1,128]{0,1:T(8,128)S(1)}, u32[]{:S(2)}, u32[]{:S(2)}) collective-permute-start(f32[1,128]{0,1:T(8,128)S(1)} %get-tuple-element.82), channel_id=1, source_target_pairs={{2,0},{4,2},{6,4},{8,6},{10,8},{12,10},{14,12},{3,1},{5,3},{7,5},{... | collective-permute-start | bytes 1544 | tf_op jit(solution)/shard_map/ppermute | solution.py:27
  198.5 85.2 %copy-start.10 = (f32[16,65,130]{1,2,0:T(8,128)S(1)}, f32[16,65,130]{1,2,0:T(8,128)}, u32[]{:S(2)}) copy-start(f32[16,65,130]{1,2,0:T(8,128)} %get-tuple-element.44) | copy-start | bytes 1622404
  198.5 85.2 %copy-start.11 = (f32[16,65,130]{1,2,0:T(8,128)S(1)}, f32[16,65,130]{1,2,0:T(8,128)}, u32[]{:S(2)}) copy-start(f32[16,65,130]{1,2,0:T(8,128)} %get-tuple-element.51) | copy-start | bytes 1622404
  198.6 6.6 %collective-permute-start.12 = (f32[1,128]{0,1:T(8,128)S(1)}, f32[1,128]{0,1:T(8,128)S(1)}, u32[]{:S(2)}, u32[]{:S(2)}) collective-permute-start(f32[1,128]{0,1:T(8,128)S(1)} %get-tuple-element.81), channel_id=1, source_target_pairs={{0,2},{2,4},{4,6},{6,8},{8,10},{10,12},{12,14},{1,3},{3,5},{5,7},{... | collective-permute-start | bytes 1544 | tf_op jit(solution)/shard_map/ppermute | solution.py:25
  205.2 4.3 %collective-permute-start.15 = (f32[66,1]{0,1:T(1,128)S(1)}, f32[66,1]{0,1:T(1,128)S(1)}, u32[]{:S(2)}, u32[]{:S(2)}) collective-permute-start(f32[66,1]{0,1:T(1,128)S(1)} %get-tuple-element.62), channel_id=1, source_target_pairs={{1,0},{3,2},{5,4},{7,6},{9,8},{11,10},{13,12},{15,14},{17,16},{19,... | collective-permute-start | bytes 800 | tf_op jit(solution)/shard_map/ppermute | solution.py:27
  206.5 3.8 %collective-permute-start.14 = (f32[66,1]{0,1:T(1,128)S(1)}, f32[66,1]{0,1:T(1,128)S(1)}, u32[]{:S(2)}, u32[]{:S(2)}) collective-permute-start(f32[66,1]{0,1:T(1,128)S(1)} %get-tuple-element.61), channel_id=1, source_target_pairs={{0,1},{2,3},{4,5},{6,7},{8,9},{10,11},{12,13},{14,15},{16,17},{18,... | collective-permute-start | bytes 800 | tf_op jit(solution)/shard_map/ppermute | solution.py:25
  277.7 11.3 %collective-permute-start.17 = (f32[1,128]{0,1:T(8,128)S(1)}, f32[1,128]{0,1:T(8,128)S(1)}, u32[]{:S(2)}, u32[]{:S(2)}) collective-permute-start(f32[1,128]{0,1:T(8,128)S(1)} %get-tuple-element.80), channel_id=1, source_target_pairs={{2,0},{4,2},{6,4},{8,6},{10,8},{12,10},{14,12},{3,1},{5,3},{7,5},{... | collective-permute-start | bytes 1544 | tf_op jit(solution)/shard_map/ppermute | solution.py:27
  279.0 10.0 %collective-permute-start.16 = (f32[1,128]{0,1:T(8,128)S(1)}, f32[1,128]{0,1:T(8,128)S(1)}, u32[]{:S(2)}, u32[]{:S(2)}) collective-permute-start(f32[1,128]{0,1:T(8,128)S(1)} %get-tuple-element.79), channel_id=1, source_target_pairs={{0,2},{2,4},{4,6},{6,8},{8,10},{10,12},{12,14},{1,3},{3,5},{5,7},{... | collective-permute-start | bytes 1544 | tf_op jit(solution)/shard_map/ppermute | solution.py:25
  289.0 7.9 %copy-start.18 = (f32[16,64,128]{1,2,0:T(8,128)S(1)}, f32[16,64,128]{1,2,0:T(8,128)}, u32[]{:S(2)}) copy-start(f32[16,64,128]{1,2,0:T(8,128)} %get-tuple-element.35) | copy-start | bytes 1572868
  290.2 9.0 %collective-permute-start.19 = (f32[66,1]{0,1:T(1,128)S(1)}, f32[66,1]{0,1:T(1,128)S(1)}, u32[]{:S(2)}, u32[]{:S(2)}) collective-permute-start(f32[66,1]{0,1:T(1,128)S(1)} %get-tuple-element.60), channel_id=1, source_target_pairs={{1,0},{3,2},{5,4},{7,6},{9,8},{11,10},{13,12},{15,14},{17,16},{19,... | collective-permute-start | bytes 800 | tf_op jit(solution)/shard_map/ppermute | solution.py:27
  291.5 7.7 %collective-permute-start.18 = (f32[66,1]{0,1:T(1,128)S(1)}, f32[66,1]{0,1:T(1,128)S(1)}, u32[]{:S(2)}, u32[]{:S(2)}) collective-permute-start(f32[66,1]{0,1:T(1,128)S(1)} %get-tuple-element.59), channel_id=1, source_target_pairs={{0,1},{2,3},{4,5},{6,7},{8,9},{10,11},{12,13},{14,15},{16,17},{18,... | collective-permute-start | bytes 800 | tf_op jit(solution)/shard_map/ppermute | solution.py:25
  296.9 1.2 copy-start.17
  298.1 1.1 copy-start.32
  298.1 1.1 copy-start.34
  298.1 1.3 copy-start.21
  299.2 33.3 %copy-start.40 = (f32[64,128]{0,1:T(8,128)S(1)}, f32[64,128]{0,1:T(8,128)}, u32[]{:S(2)}) copy-start(f32[64,128]{0,1:T(8,128)} %get-tuple-element.25) | copy-start | bytes 98308
  (5 other events, 3.7 us)
where the time goes:
time: 335 us; the launch traced here: 333 us
  blocking collectives  156 us (47%)
  other arithmetic  64.2 us (19%)
  starting transfers between devices  54.1 us (16%)
  local copies, waits for them, and re-layouts  37.3 us (11%)
  waiting for transfers between devices  12.8 us (4%)
  between operations  8.36 us (2%)
    psum x3, blocking collectives, norm_sum(): return lax.psum(jnp.sum(values), ('gx', 'gy'))  95.5 us
    psum x2, blocking collectives, curvature_sum(): return lax.psum(jnp.sum(values), ('gx', 'gy'))  60.5 us
    ppermute x10, starting transfers between devices, with_halo(): lax.ppermute(tail, axis, [(i, (i + 1) % count) for i in range(ends)])  41.2 us
    unnamed x109, local copies, waits for them, and re-layouts  15.7 us
    mul x1, other arithmetic, stratified_advance(): 0.25 * (meridional_inner[:, :, 1:] + meridional_inner[:, :, :-1])  13.1 us
    ppermute x10, starting transfers between devices, with_halo(): lax.ppermute(head, axis, [((i + 1) % count, i) for i in range(ends)])  12.9 us
    ppermute x10, waiting for transfers between devices, with_halo(): lax.ppermute(tail, axis, [(i, (i + 1) % count) for i in range(ends)])  9.93 us
    mul x6, other arithmetic, diffuse(): flux_column = column_faces * (values[..., :, 1:] - values[..., :, :-1])  7.72 us
  transfers between devices with their start and end apart: 20, of which 9 were waited for; matrix products, arithmetic and copies ran while one was open for 5% of the time, Pallas kernels for 0%

commit v1 on v0

v1 whole, which is shorter than its diff:
```python
import functools

import jax
import jax.numpy as jnp
from jax import lax
from jax.experimental import pallas as pl
from jax.experimental.pallas import tpu as pltpu
from jax.sharding import PartitionSpec as P

TS = 64
ITERS = 3
CHUNKS = 4
HALO = 8

pressure_coef = 0.02
biharmonic_coef = 0.02
advection_coef = 0.5
surface_coef = 0.5
divergence_coef = 0.1

MESH = pl.DeviceIdType.MESH


def kernel(
    count,
    u_ref, v_ref, t_ref, spin_ref, thick_ref, visc_ref, depth_ref, sea_ref, wet_ref,
    ou_ref, ov_ref, ot_ref, ox_ref, or_ref,
    own, own2, buf, buf2, res, res2, weights, total, gathered,
    load_sem, load2_sem, local_sem, swap_send, swap_recv, halo_send, halo_recv,
    out_sem, back_send, back_recv, gram_send, gram_recv,
):
    levels, rows, columns = u_ref.shape
    half = rows // 2
    span = half + 2 * HALO
    reach = half + HALO
    per = levels // CHUNKS
    group = lax.axis_index("group")
    gx = lax.axis_index("gx")
    core = lax.axis_index("gy")
    other = 1 - core
    peers = 2 * count
    me = gx * 2 + core

    barrier = pltpu.get_barrier_semaphore()

    def greet(k, _):
        peer = lax.rem(me + k, peers)
        pl.semaphore_signal(
            barrier, inc=1, device_id=(group, peer // 2, lax.rem(peer, 2)), device_id_type=MESH
        )
        return 0

    lax.fori_loop(1, peers, greet, 0)

    def loads(k):
        part = pl.ds(k * per, per)
        return [
            pltpu.make_async_copy(ref.at[part], own.at[f, part], load_sem.at[f, k])
            for f, ref in enumerate((u_ref, v_ref, t_ref))
        ]

    flat_loads = [
        pltpu.make_async_copy(ref, own2.at[f], load2_sem.at[f])
        for f, ref in enumerate((visc_ref, depth_ref, sea_ref))
    ]
    for copy in flat_loads:
        copy.start()
    for k in range(CHUNKS):
        for copy in loads(k):
            copy.start()

    spin_row = jnp.broadcast_to(spin_ref[...], (rows, rows))
    diagonal = lax.broadcasted_iota(jnp.int32, (rows, rows), 0) == lax.broadcasted_iota(
        jnp.int32, (rows, rows), 1
    )
    spin_column = jnp.sum(jnp.where(diagonal, spin_row, 0.0), axis=1, keepdims=True)
    own2[3] = jnp.broadcast_to(spin_column, (rows, columns))

    first = gx == 0
    last = gx == count - 1

    def clear(start):
        def one(l, _):
            for h in range(2):
                for f in range(3):
                    buf[h, f, l, start : start + HALO, :] = jnp.zeros((HALO, columns), jnp.float32)
            return 0

        lax.fori_loop(0, levels, one, 0)
        for h in range(2):
            for f in range(4):
                buf2[h, f, start : start + HALO, :] = jnp.zeros((HALO, columns), jnp.float32)

    @pl.when(jnp.logical_and(first, core == 0))
    def _():
        clear(0)

    @pl.when(jnp.logical_and(last, core == 1))
    def _():
        clear(HALO + half)

    pl.semaphore_wait(barrier, peers - 1)

    def source(k, where):
        if k is None:
            return own2.at[:, where, :]
        return own.at[:, pl.ds(k * per, per), where, :]

    def target(k, which, where):
        if k is None:
            return buf2.at[which, :, where, :]
        return buf.at[which, :, pl.ds(k * per, per), where, :]

    def slot(k):
        return CHUNKS if k is None else k

    def taken(c):
        return pl.ds(pl.multiple_of((half - HALO) * c, 8), reach)

    def placed(c):
        return pl.ds(pl.multiple_of(HALO - HALO * c, 8), reach)

    def swap(k):
        return pltpu.make_async_remote_copy(
            src_ref=source(k, taken(other)),
            dst_ref=target(k, core, placed(other)),
            send_sem=swap_send.at[slot(k)],
            recv_sem=swap_recv.at[slot(k)],
            device_id=(group, gx, other),
            device_id_type=MESH,
        )

    def keep(k):
        return pltpu.make_async_copy(
            source(k, taken(core)), target(k, core, placed(core)), local_sem.at[slot(k)]
        )

    def halo_down(k):
        return pltpu.make_async_remote_copy(
            src_ref=source(k, pl.ds(rows - HALO, HALO)),
            dst_ref=target(k, core, pl.ds(0, HALO)),
            send_sem=halo_send.at[0, slot(k)],
            recv_sem=halo_recv.at[core, slot(k)],
            device_id=(group, lax.rem(gx + 1, count), 0),
            device_id_type=MESH,
        )

    def halo_up(k):
        return pltpu.make_async_remote_copy(
            src_ref=source(k, pl.ds(0, HALO)),
            dst_ref=target(k, core, pl.ds(HALO + half, HALO)),
            send_sem=halo_send.at[1, slot(k)],
            recv_sem=halo_recv.at[core, slot(k)],
            device_id=(group, lax.rem(gx + count - 1, count), 1),
            device_id_type=MESH,
        )

    def halo_in(k, h):
        return pltpu.make_async_remote_copy(
            src_ref=source(k, pl.ds(0, HALO)),
            dst_ref=target(k, h, pl.ds(0, HALO)),
            send_sem=halo_send.at[0, slot(k)],
            recv_sem=halo_recv.at[h, slot(k)],
            device_id=(group, gx, other),
            device_id_type=MESH,
        )

    has_outer = jnp.where(core == 0, gx > 0, gx < count - 1)

    def send(k):
        @pl.when(gx < count - 1)
        def _():
            halo_down(k).start()

        @pl.when(gx > 0)
        def _():
            halo_up(k).start()

        swap(k).start()
        keep(k).start()

    def arrive(k):
        keep(k).wait()
        swap(k).wait_recv()

        @pl.when(has_outer)
        def _():
            halo_in(k, 0).wait_recv()
            halo_in(k, 1).wait_recv()

    def sent(k):
        swap(k).wait_send()

        @pl.when(gx < count - 1)
        def _():
            halo_down(k).wait_send()

        @pl.when(gx > 0)
        def _():
            halo_up(k).wait_send()

    for copy in flat_loads:
        copy.wait()
    send(None)
    for k in range(CHUNKS):
        for copy in loads(k):
            copy.wait()
        send(k)

    lane = lax.broadcasted_iota(jnp.int32, (span, columns), 1)
    row = lax.broadcasted_iota(jnp.int32, (span, columns), 0)
    at_left = lane == 0
    at_right = lane == columns - 1

    def up(a):
        return pltpu.roll(a, 1, 0)

    def down(a):
        return pltpu.roll(a, span - 1, 0)

    def left(pair):
        r0, r1 = [pltpu.roll(a, 1, 1) for a in pair]
        return [jnp.where(at_left, 0.0, r0), jnp.where(at_left, r0, r1)]

    def right(pair):
        r0, r1 = [pltpu.roll(a, columns - 1, 1) for a in pair]
        return [jnp.where(at_right, r1, r0), jnp.where(at_right, 0.0, r1)]

    def around(pair):
        return [up(a) for a in pair], [down(a) for a in pair], left(pair), right(pair)

    outer_tile = jnp.where(core == 0, gx - 1, gx + 1)
    outer_tile_safe = jnp.clip(outer_tile, 0, count - 1)
    outer_flag = jnp.where(has_outer, 1, 0)
    in_outer = jnp.where(core == 0, row, span - 1 - row) < HALO
    mask = []
    for h in range(2):
        inner = jnp.where(lane < TS, wet_ref[gx, 2 * h], wet_ref[gx, 2 * h + 1])
        outer = jnp.where(
            lane < TS,
            wet_ref[outer_tile_safe, 2 * h] * outer_flag,
            wet_ref[outer_tile_safe, 2 * h + 1] * outer_flag,
        )
        mask.append(jnp.where(in_outer, outer, inner).astype(jnp.float32))
    sides = around(mask)
    for h in range(2):
        m = mask[h]
        mu, md, ml, mr = [side[h] for side in sides]
        number = mu + md + ml + mr
        weights[h, 0] = m
        weights[h, 1] = number
        weights[h, 2] = mu
        weights[h, 3] = md
        weights[h, 4] = ml
        weights[h, 5] = mr
        weights[h, 6] = mu - md
        weights[h, 7] = ml - mr

    arrive(None)

    def face_weights(pair):
        ring = around(pair)
        result = []
        for h in range(2):
            four = [
                0.5 * (pair[h] + ring[side][h]) * mask[h] * sides[side][h] for side in range(4)
            ]
            result.append(four)
        return result

    viscous = face_weights([buf2[0, 0], buf2[1, 0]])
    for h in range(2):
        for side in range(4):
            weights[h, 8 + side] = viscous[h][side]
        weights[h, 12] = viscous[h][0] + viscous[h][1] + viscous[h][2] + viscous[h][3]

    for h in range(2):
        for i in range(4):
            total[h, i] = jnp.zeros((span, columns), jnp.float32)

    def level(l, _):
        thickness = thick_ref[l]
        fields = []
        rings = []
        for f in range(3):
            pair = [buf[h, f, l] * weights[h, 0] for h in range(2)]
            fields.append(pair)
            rings.append(around(pair))
        u, v, t = fields
        viscous_part = []
        for f in range(3):
            viscous_part.append(
                [
                    weights[h, 8] * rings[f][0][h]
                    + weights[h, 9] * rings[f][1][h]
                    + (weights[h, 10] * rings[f][2][h] + weights[h, 11] * rings[f][3][h])
                    - weights[h, 12] * fields[f][h]
                    for h in range(2)
                ]
            )
        hyper = []
        for f in range(2):
            once = [
                weights[h, 0]
                * (
                    (rings[f][0][h] + rings[f][1][h])
                    + (rings[f][2][h] + rings[f][3][h])
                    - weights[h, 1] * fields[f][h]
                )
                for h in range(2)
            ]
            ring = around(once)
            hyper.append(
                [
                    (ring[0][h] + ring[1][h]) + (ring[2][h] + ring[3][h]) - weights[h, 1] * once[h]
                    for h in range(2)
                ]
            )
        tu, td, tl, tr = rings[2]
        uu, ud, _, _ = rings[0]
        _, _, vl, vr = rings[1]
        for h in range(2):
            m = weights[h, 0]
            slope_row = thickness * (td[h] - tu[h] + weights[h, 6] * t[h])
            slope_column = thickness * (tr[h] - tl[h] + weights[h, 7] * t[h])
            sum_row = total[h, 2] + slope_row
            sum_column = total[h, 3] + slope_column
            total[h, 2] = sum_row
            total[h, 3] = sum_column
            grad_row = sum_row - 0.5 * slope_row
            grad_column = sum_column - 0.5 * slope_column
            spread = (
                weights[h, 3] * ((u[h] + ud[h]) * (t[h] + td[h]))
                - weights[h, 2] * ((u[h] + uu[h]) * (t[h] + tu[h]))
                + (
                    weights[h, 5] * ((v[h] + vr[h]) * (t[h] + tr[h]))
                    - weights[h, 4] * ((v[h] + vl[h]) * (t[h] + tl[h]))
                )
            )
            spin = buf2[h, 3]
            u_next = m * (
                u[h]
                + spin * v[h]
                - (0.5 * pressure_coef) * grad_row
                + viscous_part[0][h]
                - biharmonic_coef * hyper[0][h]
            )
            v_next = m * (
                v[h]
                - spin * u[h]
                - (0.5 * pressure_coef) * grad_column
                + viscous_part[1][h]
                - biharmonic_coef * hyper[1][h]
            )
            t_next = m * (t[h] - (0.25 * advection_coef) * spread + viscous_part[2][h])
            total[h, 0] += thickness * u_next
            total[h, 1] += thickness * v_next
            res[h, 0, l] = u_next[HALO : HALO + half]
            res[h, 1, l] = v_next[HALO : HALO + half]
            res[h, 2, l] = t_next[HALO : HALO + half]
        return 0

    mine = pl.ds(pl.multiple_of(half * core, 8), half)

    def outs(k):
        part = pl.ds(k * per, per)
        local = [
            pltpu.make_async_copy(
                res.at[core, f, part], ref.at[part, mine, :], out_sem.at[f, k]
            )
            for f, ref in enumerate((ou_ref, ov_ref, ot_ref))
        ]
        remote = [
            pltpu.make_async_remote_copy(
                src_ref=res.at[other, f, part],
                dst_ref=ref.at[part, mine, :],
                send_sem=back_send.at[f, k],
                recv_sem=back_recv.at[f, k],
                device_id=(group, gx, other),
                device_id_type=MESH,
            )
            for f, ref in enumerate((ou_ref, ov_ref, ot_ref))
        ]
        return remote + local

    def chunk(k, _):
        arrive(k)
        lax.fori_loop(k * per, (k + 1) * per, level, 0)
        for copy in outs(k):
            copy.start()
        return 0

    lax.fori_loop(0, CHUNKS, chunk, 0)

    face = face_weights([buf2[0, 1], buf2[1, 1]])
    scaling = [
        surface_coef + (face[h][0] + face[h][1]) + (face[h][2] + face[h][3]) for h in range(2)
    ]
    inverse = [1.0 / scaling[h] for h in range(2)]
    flow_u = [total[h, 0] for h in range(2)]
    flow_v = [total[h, 1] for h in range(2)]
    before, after = left(flow_v), right(flow_v)
    vectors = [
        [
            mask[h]
            * (
                surface_coef * buf2[h, 2]
                - (0.5 * divergence_coef)
                * ((down(flow_u[h]) - up(flow_u[h])) + (after[h] - before[h]))
            )
            * inverse[h]
            for h in range(2)
        ]
    ]
    for _ in range(ITERS):
        ring = around(vectors[-1])
        vectors.append(
            [
                (
                    (face[h][0] * ring[0][h] + face[h][1] * ring[1][h])
                    + (face[h][2] * ring[2][h] + face[h][3] * ring[3][h])
                )
                * inverse[h]
                for h in range(2)
            ]
        )
    inside = slice(HALO, HALO + half)
    basis = [[pair[h][inside] for h in range(2)] for pair in vectors]
    scale = [scaling[h][inside] for h in range(2)]

    def dot(a, b):
        both = scale[0] * a[0] * b[0] + scale[1] * a[1] * b[1]
        return jnp.sum(both, axis=0, keepdims=True)

    moments = 2 * ITERS - 1
    difference = [
        [basis[k][h] - basis[k + 1][h] for h in range(2)] for k in range(ITERS)
    ]
    gathered[me] = jnp.zeros(gathered.shape[1:], jnp.float32)
    lines = [dot(basis[(k + 1) // 2], basis[k // 2]) for k in range(moments)]
    lines += [dot(basis[(k + 1) // 2], difference[k // 2]) for k in range(moments)]
    for k, line in enumerate(lines):
        gathered[me, k : k + 1, :] = line

    def gram(k):
        peer = lax.rem(me + k, peers)
        return pltpu.make_async_remote_copy(
            src_ref=gathered.at[me],
            dst_ref=gathered.at[me],
            send_sem=gram_send.at[k],
            recv_sem=gram_recv.at[me],
            device_id=(group, peer // 2, lax.rem(peer, 2)),
            device_id_type=MESH,
        )

    def gram_from(k):
        peer = lax.rem(me + k, peers)
        return pltpu.make_async_remote_copy(
            src_ref=gathered.at[peer],
            dst_ref=gathered.at[peer],
            send_sem=gram_send.at[k],
            recv_sem=gram_recv.at[peer],
            device_id=(group, peer // 2, lax.rem(peer, 2)),
            device_id_type=MESH,
        )

    def gram_start(k, _):
        gram(k).start()
        return 0

    def gram_wait(k, _):
        gram_from(k).wait_recv()
        return 0

    def gram_sent(k, _):
        gram(k).wait_send()
        return 0

    lax.fori_loop(1, peers, gram_start, 0)
    lax.fori_loop(1, peers, gram_wait, 0)

    summed = lax.fori_loop(
        0, peers, lambda k, acc: acc + gathered[k], jnp.zeros(gathered.shape[1:], jnp.float32)
    )
    sums = jnp.sum(summed, axis=1, keepdims=True)
    mass = [sums[k : k + 1] for k in range(moments)]
    stiff = [sums[moments + k : moments + k + 1] for k in range(moments)]

    def quadratic(coefs, table):
        value = None
        for i, a in enumerate(coefs):
            for j, b in enumerate(coefs):
                term = a * b * table[i + j]
                value = term if value is None else value + term
        return value

    one = jnp.ones((1, 1), jnp.float32)
    zero = jnp.zeros((1, 1), jnp.float32)
    remains = [one]
    heading = [one]
    guess = [zero] * ITERS
    rho = mass[0]
    for iteration in range(ITERS):
        step = rho / quadratic(heading, stiff)
        for j, c in enumerate(heading):
            guess[j] = guess[j] + step * c
        moved = remains + [zero]
        for j, c in enumerate(heading):
            moved[j] = moved[j] - step * c
            moved[j + 1] = moved[j + 1] + step * c
        remains = moved
        if iteration + 1 < ITERS:
            rho_new = quadratic(remains, mass)
            ratio = rho_new / rho
            heading = [
                remains[j] + ratio * heading[j] if j < len(heading) else remains[j]
                for j in range(len(remains))
            ]
            rho = rho_new

    for h in range(2):
        x = guess[0] * basis[0][h]
        for j in range(1, ITERS):
            x = x + guess[j] * basis[j][h]
        r = remains[0] * basis[0][h]
        for j in range(1, ITERS + 1):
            r = r + remains[j] * basis[j][h]
        res2[h, 0] = x
        res2[h, 1] = scale[h] * r

    def flat_outs():
        k = CHUNKS
        local = [
            pltpu.make_async_copy(res2.at[core, f], ref.at[mine, :], out_sem.at[f, k])
            for f, ref in enumerate((ox_ref, or_ref))
        ]
        remote = [
            pltpu.make_async_remote_copy(
                src_ref=res2.at[other, f],
                dst_ref=ref.at[mine, :],
                send_sem=back_send.at[f, k],
                recv_sem=back_recv.at[f, k],
                device_id=(group, gx, other),
                device_id_type=MESH,
            )
            for f, ref in enumerate((ox_ref, or_ref))
        ]
        return remote + local

    for copy in flat_outs():
        copy.start()
    lax.fori_loop(1, peers, gram_sent, 0)
    sent(None)
    for k in range(CHUNKS):
        sent(k)
        for copy in outs(k):
            copy.wait()
    for copy in flat_outs():
        copy.wait()


def per_device(count, *args):
    u, v, t, spin, thick, visc, depth, sea, wet = args
    levels, rows, columns = u.shape
    half = rows // 2
    span = half + 2 * HALO
    assert rows == TS and columns == 2 * TS
    peers = 2 * count
    f32 = jnp.float32
    anywhere = pl.BlockSpec(memory_space=pl.ANY)
    vmem = pl.BlockSpec(memory_space=pltpu.VMEM)
    smem = pl.BlockSpec(memory_space=pltpu.SMEM)
    dma = pltpu.SemaphoreType.DMA
    return pl.pallas_call(
        functools.partial(kernel, count),
        out_shape=[jax.ShapeDtypeStruct(u.shape, f32)] * 3
        + [jax.ShapeDtypeStruct(sea.shape, f32)] * 2,
        in_specs=[anywhere, anywhere, anywhere, vmem, smem, anywhere, anywhere, anywhere, smem],
        out_specs=[anywhere] * 5,
        scratch_shapes=[
            pltpu.VMEM((3, levels, rows, columns), f32),
            pltpu.VMEM((4, rows, columns), f32),
            pltpu.VMEM((2, 3, levels, span, columns), f32),
            pltpu.VMEM((2, 4, span, columns), f32),
            pltpu.VMEM((2, 3, levels, half, columns), f32),
            pltpu.VMEM((2, 2, half, columns), f32),
            pltpu.VMEM((2, 13, span, columns), f32),
            pltpu.VMEM((2, 4, span, columns), f32),
            pltpu.VMEM((peers, 16, columns), f32),
            dma((3, CHUNKS)),
            dma((3,)),
            dma((CHUNKS + 1,)),
            dma((CHUNKS + 1,)),
            dma((CHUNKS + 1,)),
            dma((2, CHUNKS + 1)),
            dma((2, CHUNKS + 1)),
            dma((3, CHUNKS + 1)),
            dma((3, CHUNKS + 1)),
            dma((3, CHUNKS + 1)),
            dma((peers,)),
            dma((peers,)),
        ],
        compiler_params=pltpu.CompilerParams(
            collective_id=0, has_side_effects=True, vmem_limit_bytes=32 * 1024 * 1024
        ),
    )(u, v, t, spin.reshape(1, rows), thick, visc, depth, sea, wet)


def solution(mesh):
    cells = P(None, ("group", "gx"), "gy")
    flat = P(("group", "gx"), "gy")
    assert mesh.shape["gy"] == 2
    return jax.shard_map(
        functools.partial(per_device, mesh.shape["gx"]),
        mesh=mesh,
        in_specs=(cells, cells, cells, P("gx"), P(), P("gx", "gy"), P("gx", "gy"), flat, P()),
        out_specs=(cells, cells, cells, flat, flat),
        check_vma=False,
    )
```

time: 335 us -> 36.3 us (0.11)
  blocking collectives: 156 us -> 0 us
  other arithmetic: 64.2 us -> 0 us
  starting transfers between devices: 54.1 us -> 0 us
  local copies, waits for them, and re-layouts: 37.3 us -> 9.78 us
  Pallas kernels: 0 us -> 25.4 us
  waiting for transfers between devices: 12.8 us -> 0 us
  between operations: 8.36 us -> 0.67 us
    psum x5 -> x0, blocking collectives: 156 us -> none  [the longest x3 95.5 us: norm_sum(): return lax.psum(jnp.sum(values), ('gx', 'gy'))]
    ppermute x20 -> x0, starting transfers between devices: 54.1 us -> none  [the longest x10 41.2 us: with_halo(): lax.ppermute(tail, axis, [(i, (i + 1) % count) for i in range(ends)])]
    mul x21 -> x0, other arithmetic: 35.5 us -> none  [the longest x1 13.1 us: stratified_advance(): 0.25 * (meridional_inner[:, :, 1:] + meridional_inner[:, :, :-1])]
    pallas_call x0 -> x1, Pallas kernels: none -> 25.4 us  [per_device(): pl.pallas_call(functools.partial(kernel, count), out_shape=[jax.ShapeDtyp...]
    ppermute x20 -> x0, waiting for transfers between devices: 12.8 us -> none  [the longest x10 9.93 us: with_halo(): lax.ppermute(tail, axis, [(i, (i + 1) % count) for i in range(ends)])]
    reduce_sum x6 -> x0, other arithmetic: 12.8 us -> none  [the longest x1 7.2 us: per_device(): transport_u = jnp.sum(easting_current_next * thickness, axis=0)]
    slice x10 -> x0, local copies, waits for them, and re-layouts: 11.2 us -> none  [the longest x6 6.18 us: with_halo(): lax.slice_in_dim(cells, cells.shape[dim] - width, cells.shape[dim], axis=...]
    concatenate x6 -> x0, other arithmetic: 6.41 us -> none  [the longest x5 6.16 us: with_halo(): jnp.concatenate([lax.ppermute(tail, axis, [(i, (i + 1) % count) for i in...]
  transfers between devices with their start and end apart: 20 -> 0, of which waited for: 9 -> 0; matrix products, arithmetic and copies ran while one was open for 5% -> 0% of each run, Pallas kernels for 0% -> 0%
where the time goes in v1:
time: 36.3 us; the launch traced here: 35.8 us
  Pallas kernels  25.4 us (70%)
  local copies, waits for them, and re-layouts  9.78 us (27%)
  between operations  0.67 us (2%)
    pallas_call x1, Pallas kernels, per_device(): pl.pallas_call(functools.partial(kernel, count), out_shape=[jax.ShapeDtyp...  25.4 us
    unnamed x22, local copies, waits for them, and re-layouts  9.78 us

profile of v1, /device:TPU:0, one launch (start us, length us, event | category | flops | bytes accessed | tf_op | source)
XLA Modules:
  0.0 35.8 jit_solution(16392083474953853667)
XLA Ops:
  0.6 0.0 copy-start.6
  0.6 0.0 copy-start.7
  0.7 0.8 %copy.14.wet_ref = s32[8,4]{1,0:T(8,128)S(1)} copy(s32[8,4]{0,1:T(4,128)} %param.17) | data formatting | bytes 256 | tf_op args[8]
  1.4 0.0 copy-done.6
  1.4 0.0 copy-done.7
  1.4 0.0 copy-start
  1.4 1.0 %copy-done = f32[16,64,128]{2,1,0:T(8,128)S(1)} copy-done((f32[16,64,128]{2,1,0:T(8,128)S(1)}, f32[16,64,128]{2,1,0:T(8,128)}, u32[]{:S(2)}) %copy-start) | copy-done | bytes 524312
  2.5 0.0 copy-start.1
  2.5 1.0 %copy-done.1 = f32[16,64,128]{2,1,0:T(8,128)S(1)} copy-done((f32[16,64,128]{2,1,0:T(8,128)S(1)}, f32[16,64,128]{2,1,0:T(8,128)}, u32[]{:S(2)}) %copy-start.1) | copy-done | bytes 524312
  3.5 0.0 copy-start.2
  3.5 1.0 %copy-done.2 = f32[16,64,128]{2,1,0:T(8,128)S(1)} copy-done((f32[16,64,128]{2,1,0:T(8,128)S(1)}, f32[16,64,128]{2,1,0:T(8,128)}, u32[]{:S(2)}) %copy-start.2) | copy-done | bytes 524312
  4.6 0.0 copy-start.3
  4.6 0.8 %copy-done.3 = f32[64,128]{1,0:T(8,128)S(1)} copy-done((f32[64,128]{1,0:T(8,128)S(1)}, f32[64,128]{1,0:T(8,128)}, u32[]{:S(2)}) %copy-start.3) | copy-done | bytes 32792
  5.3 0.0 copy-start.4
  5.3 0.8 %copy-done.4 = f32[64,128]{1,0:T(8,128)S(1)} copy-done((f32[64,128]{1,0:T(8,128)S(1)}, f32[64,128]{1,0:T(8,128)}, u32[]{:S(2)}) %copy-start.4) | copy-done | bytes 32792
  6.1 0.0 copy-start.5
  6.1 0.8 %copy-done.5 = f32[64,128]{1,0:T(8,128)S(1)} copy-done((f32[64,128]{1,0:T(8,128)S(1)}, f32[64,128]{1,0:T(8,128)}, u32[]{:S(2)}) %copy-start.5) | copy-done | bytes 32792
  6.8 25.4 %shard_map.128 = (f32[16,64,128]{2,1,0:T(8,128)S(1)}, f32[16,64,128]{2,1,0:T(8,128)S(1)}, f32[16,64,128]{2,1,0:T(8,128)S(1)}, f32[64,128]{1,0:T(8,128)S(1)}, f32[64,128]{1,0:T(8,128)S(1)}) custom-call(f32[16,64,128]{2,1,0:T(8,128)S(1)} %copy-done, f32[16,64,128]{2,1,0:T(8,128)S(1)} %copy-done.1, f32[16,64,128]{2,1,0:T(8,128)S(1)} %copy-done.2, ...), custom_call_target="tpu_custom_call" | custom-call | tf_op jit(solution)/shard_map/pallas_call | solution.py:574
  32.2 0.8 %copy.20 = f32[16,64,128]{2,1,0:T(8,128)} copy(f32[16,64,128]{2,1,0:T(8,128)S(1)} %get-tuple-element.10) | data formatting | bytes 1048576
  33.0 0.8 %copy.21 = f32[16,64,128]{2,1,0:T(8,128)} copy(f32[16,64,128]{2,1,0:T(8,128)S(1)} %get-tuple-element.11) | data formatting | bytes 1048576
  33.8 0.8 %copy.22 = f32[16,64,128]{2,1,0:T(8,128)} copy(f32[16,64,128]{2,1,0:T(8,128)S(1)} %get-tuple-element.12) | data formatting | bytes 1048576
  34.6 0.6 %copy.23 = f32[64,128]{1,0:T(8,128)} copy(f32[64,128]{1,0:T(8,128)S(1)} %get-tuple-element.13) | data formatting | bytes 65536
  35.2 0.6 %copy.24 = f32[64,128]{1,0:T(8,128)} copy(f32[64,128]{1,0:T(8,128)S(1)} %get-tuple-element.14) | data formatting | bytes 65536
Async XLA Ops:
  0.6 0.8 %copy-start.6 = (f32[64]{0:T(128)S(1)}, f32[64]{0:T(128)}, u32[]{:S(2)}) copy-start(f32[64]{0:T(128)} %param.12) | copy-start | bytes 772
  0.6 0.8 %copy-start.7 = (f32[16]{0:T(128)S(1)}, f32[16]{0:T(128)}, u32[]{:S(2)}) copy-start(f32[16]{0:T(128)} %thick_ref.1) | copy-start | bytes 196
  1.4 1.0 %copy-start = (f32[16,64,128]{2,1,0:T(8,128)S(1)}, f32[16,64,128]{2,1,0:T(8,128)}, u32[]{:S(2)}) copy-start(f32[16,64,128]{2,1,0:T(8,128)} %u_ref.1) | copy-start | bytes 1572868
  2.5 1.0 %copy-start.1 = (f32[16,64,128]{2,1,0:T(8,128)S(1)}, f32[16,64,128]{2,1,0:T(8,128)}, u32[]{:S(2)}) copy-start(f32[16,64,128]{2,1,0:T(8,128)} %v_ref.1) | copy-start | bytes 1572868
  3.5 1.0 %copy-start.2 = (f32[16,64,128]{2,1,0:T(8,128)S(1)}, f32[16,64,128]{2,1,0:T(8,128)}, u32[]{:S(2)}) copy-start(f32[16,64,128]{2,1,0:T(8,128)} %t_ref.1) | copy-start | bytes 1572868
  4.6 0.8 %copy-start.3 = (f32[64,128]{1,0:T(8,128)S(1)}, f32[64,128]{1,0:T(8,128)}, u32[]{:S(2)}) copy-start(f32[64,128]{1,0:T(8,128)} %visc_ref.1) | copy-start | bytes 98308
  5.3 0.8 %copy-start.4 = (f32[64,128]{1,0:T(8,128)S(1)}, f32[64,128]{1,0:T(8,128)}, u32[]{:S(2)}) copy-start(f32[64,128]{1,0:T(8,128)} %depth_ref.1) | copy-start | bytes 98308
  6.1 0.8 %copy-start.5 = (f32[64,128]{1,0:T(8,128)S(1)}, f32[64,128]{1,0:T(8,128)}, u32[]{:S(2)}) copy-start(f32[64,128]{1,0:T(8,128)} %sea_ref.1) | copy-start | bytes 98308

commit v2 on v1

--- a/solution.py
+++ b/solution.py
@@ -11,6 +11,7 @@
 ITERS = 3
 CHUNKS = 4
 HALO = 8
+VMEM_BYTES = 60 * 1024 * 1024
 
 pressure_coef = 0.02
 biharmonic_coef = 0.02
@@ -25,8 +26,8 @@
     count,
     u_ref, v_ref, t_ref, spin_ref, thick_ref, visc_ref, depth_ref, sea_ref, wet_ref,
     ou_ref, ov_ref, ot_ref, ox_ref, or_ref,
-    own, own2, buf, buf2, res, res2, weights, total, gathered,
-    load_sem, load2_sem, local_sem, swap_send, swap_recv, halo_send, halo_recv,
+    own_spin, buf, buf2, res, res2, weights, total, gathered,
+    local_sem, swap_send, swap_recv, halo_send, halo_recv,
     out_sem, back_send, back_recv, gram_send, gram_recv,
 ):
     levels, rows, columns = u_ref.shape
@@ -52,30 +53,133 @@
 
     lax.fori_loop(1, peers, greet, 0)
 
-    def loads(k):
-        part = pl.ds(k * per, per)
-        return [
-            pltpu.make_async_copy(ref.at[part], own.at[f, part], load_sem.at[f, k])
-            for f, ref in enumerate((u_ref, v_ref, t_ref))
-        ]
-
-    flat_loads = [
-        pltpu.make_async_copy(ref, own2.at[f], load2_sem.at[f])
-        for f, ref in enumerate((visc_ref, depth_ref, sea_ref))
-    ]
-    for copy in flat_loads:
-        copy.start()
-    for k in range(CHUNKS):
-        for copy in loads(k):
-            copy.start()
-
     spin_row = jnp.broadcast_to(spin_ref[...], (rows, rows))
     diagonal = lax.broadcasted_iota(jnp.int32, (rows, rows), 0) == lax.broadcasted_iota(
         jnp.int32, (rows, rows), 1
     )
     spin_column = jnp.sum(jnp.where(diagonal, spin_row, 0.0), axis=1, keepdims=True)
-    own2[3] = jnp.broadcast_to(spin_column, (rows, columns))
-
+    own_spin[...] = jnp.broadcast_to(spin_column, (rows, columns))
+
+    def taken(c):
+        return pl.ds(pl.multiple_of((half - HALO) * c, 8), reach)
+
+    def placed(c):
+        return pl.ds(pl.multiple_of(HALO - HALO * c, 8), reach)
+
+    has_outer = jnp.where(core == 0, gx > 0, gx < count - 1)
+    cells = (u_ref, v_ref, t_ref)
+    flats = (visc_ref, depth_ref, sea_ref, own_spin)
+
+    def source(f, k, where):
+        if k is None:
+            return flats[f].at[where, :]
+        return cells[f].at[pl.ds(k * per, per), where, :]
+
+    def target(f, k, which, where):
+        if k is None:
+            return buf2.at[which, f, where, :]
+        return buf.at[which, f, pl.ds(k * per, per), where, :]
+
+    def slot(k):
+        return CHUNKS if k is None else k
+
+    def swap(f, k):
+        return pltpu.make_async_remote_copy(
+            src_ref=source(f, k, taken(other)),
+            dst_ref=target(f, k, core, placed(other)),
+            send_sem=swap_send.at[f, slot(k)],
+            recv_sem=swap_recv.at[f, slot(k)],
+            device_id=(group, gx, other),
+            device_id_type=MESH,
+        )
+
+    def keep(f, k):
+        return pltpu.make_async_copy(
+            source(f, k, taken(core)),
+            target(f, k, core, placed(core)),
+            local_sem.at[f, slot(k)],
+        )
+
+    def halo_down(f, k):
+        return pltpu.make_async_remote_copy(
+            src_ref=source(f, k, pl.ds(rows - HALO, HALO)),
+            dst_ref=target(f, k, core, pl.ds(0, HALO)),
+            send_sem=halo_send.at[0, f, slot(k)],
+            recv_sem=halo_recv.at[core, f, slot(k)],
+            device_id=(group, lax.rem(gx + 1, count), 0),
+            device_id_type=MESH,
+        )
+
+    def halo_up(f, k):
+        return pltpu.make_async_remote_copy(
+            src_ref=source(f, k, pl.ds(0, HALO)),
+            dst_ref=target(f, k, core, pl.ds(HALO + half, HALO)),
+            send_sem=halo_send.at[1, f, slot(k)],
+            recv_sem=halo_recv.at[core, f, slot(k)],
+            device_id=(group, lax.rem(gx + count - 1, count), 1),
+            device_id_type=MESH,
+        )
+
+    def halo_in(f, k, h):
+        return pltpu.make_async_remote_copy(
+            src_ref=source(f, k, pl.ds(0, HALO)),
+            dst_ref=target(f, k, h, pl.ds(0, HALO)),
+            send_sem=halo_send.at[0, f, slot(k)],
+            recv_sem=halo_recv.at[h, f, slot(k)],
+            device_id=(group, gx, other),
+            device_id_type=MESH,
+        )
+
+    def span_of(k):
+        return range(4) if k is None else range(3)
+
+    def send_halo(k):
+        @pl.when(gx < count - 1)
+        def _():
+            for f in span_of(k):
+                halo_down(f, k).start()
+
+        @pl.when(gx > 0)
+        def _():
+            for f in span_of(k):
+                halo_up(f, k).start()
+
+    def send_swap(k):
+        for f in range(3):
+            swap(f, k).start()
+
+    def arrive(k):
+        for f in range(3):
+            keep(f, k).wait()
+            swap(f, k).wait_recv()
+
+        @pl.when(has_outer)
+        def _():
+            for f in span_of(k):
+                halo_in(f, k, 0).wait_recv()
+                halo_in(f, k, 1).wait_recv()
+
+    def sent(k):
+        for f in range(3):
+            swap(f, k).wait_send()
+
+        @pl.when(gx < count - 1)
+        def _():
+            for f in span_of(k):
+                halo_down(f, k).wait_send()
+
+        @pl.when(gx > 0)
+        def _():
+            for f in span_of(k):
+                halo_up(f, k).wait_send()
+
+    everything = [None] + list(range(CHUNKS))
+    for k in everything:
+        for f in range(3):
+            keep(f, k).start()
+    own_rows = own_spin[taken(core), :]
+    for h in range(2):
+        buf2[h, 3, placed(core), :] = own_rows
     first = gx == 0
     last = gx == count - 1
 
@@ -100,112 +204,9 @@
         clear(HALO + half)
 
     pl.semaphore_wait(barrier, peers - 1)
-
-    def source(k, where):
-        if k is None:
-            return own2.at[:, where, :]
-        return own.at[:, pl.ds(k * per, per), where, :]
-
-    def target(k, which, where):
-        if k is None:
-            return buf2.at[which, :, where, :]
-        return buf.at[which, :, pl.ds(k * per, per), where, :]
-
-    def slot(k):
-        return CHUNKS if k is None else k
-
-    def taken(c):
-        return pl.ds(pl.multiple_of((half - HALO) * c, 8), reach)
-
-    def placed(c):
-        return pl.ds(pl.multiple_of(HALO - HALO * c, 8), reach)
-
-    def swap(k):
-        return pltpu.make_async_remote_copy(
-            src_ref=source(k, taken(other)),
-            dst_ref=target(k, core, placed(other)),
-            send_sem=swap_send.at[slot(k)],
-            recv_sem=swap_recv.at[slot(k)],
-            device_id=(group, gx, other),
-            device_id_type=MESH,
-        )
-
-    def keep(k):
-        return pltpu.make_async_copy(
-            source(k, taken(core)), target(k, core, placed(core)), local_sem.at[slot(k)]
-        )
-
-    def halo_down(k):
-        return pltpu.make_async_remote_copy(
-            src_ref=source(k, pl.ds(rows - HALO, HALO)),
-            dst_ref=target(k, core, pl.ds(0, HALO)),
-            send_sem=halo_send.at[0, slot(k)],
-            recv_sem=halo_recv.at[core, slot(k)],
-            device_id=(group, lax.rem(gx + 1, count), 0),
-            device_id_type=MESH,
-        )
-
-    def halo_up(k):
-        return pltpu.make_async_remote_copy(
-            src_ref=source(k, pl.ds(0, HALO)),
-            dst_ref=target(k, core, pl.ds(HALO + half, HALO)),
-            send_sem=halo_send.at[1, slot(k)],
-            recv_sem=halo_recv.at[core, slot(k)],
-            device_id=(group, lax.rem(gx + count - 1, count), 1),
-            device_id_type=MESH,
-        )
-
-    def halo_in(k, h):
-        return pltpu.make_async_remote_copy(
-            src_ref=source(k, pl.ds(0, HALO)),
-            dst_ref=target(k, h, pl.ds(0, HALO)),
-            send_sem=halo_send.at[0, slot(k)],
-            recv_sem=halo_recv.at[h, slot(k)],
-            device_id=(group, gx, other),
-            device_id_type=MESH,
-        )
-
-    has_outer = jnp.where(core == 0, gx > 0, gx < count - 1)
-
-    def send(k):
-        @pl.when(gx < count - 1)
-        def _():
-            halo_down(k).start()
-
-        @pl.when(gx > 0)
-        def _():
-            halo_up(k).start()
-
-        swap(k).start()
-        keep(k).start()
-
-    def arrive(k):
-        keep(k).wait()
-        swap(k).wait_recv()
-
-        @pl.when(has_outer)
-        def _():
-            halo_in(k, 0).wait_recv()
-            halo_in(k, 1).wait_recv()
-
-    def sent(k):
-        swap(k).wait_send()
-
-        @pl.when(gx < count - 1)
-        def _():
-            halo_down(k).wait_send()
-
-        @pl.when(gx > 0)
-        def _():
-            halo_up(k).wait_send()
-
-    for copy in flat_loads:
-        copy.wait()
-    send(None)
-    for k in range(CHUNKS):
-        for copy in loads(k):
-            copy.wait()
-        send(k)
+    for k in everything:
+        send_halo(k)
+        send_swap(k)
 
     lane = lax.broadcasted_iota(jnp.int32, (span, columns), 1)
     row = lax.broadcasted_iota(jnp.int32, (span, columns), 0)
@@ -235,11 +236,11 @@
     in_outer = jnp.where(core == 0, row, span - 1 - row) < HALO
     mask = []
     for h in range(2):
-        inner = jnp.where(lane < TS, wet_ref[gx, 2 * h], wet_ref[gx, 2 * h + 1])
+        inner = jnp.where(lane < TS, wet_ref[2 * h, gx], wet_ref[2 * h + 1, gx])
         outer = jnp.where(
             lane < TS,
-            wet_ref[outer_tile_safe, 2 * h] * outer_flag,
-            wet_ref[outer_tile_safe, 2 * h + 1] * outer_flag,
+            wet_ref[2 * h, outer_tile_safe] * outer_flag,
+            wet_ref[2 * h + 1, outer_tile_safe] * outer_flag,
         )
         mask.append(jnp.where(in_outer, outer, inner).astype(jnp.float32))
     sides = around(mask)
@@ -559,6 +560,32 @@
         copy.wait()
 
 
+def deliver(*refs):
+    sources, targets, held = refs[:5], refs[5:10], refs[10:15]
+    into_sem, out_sem = refs[15:]
+
+    def cut(ref, k):
+        size = ref.shape[0] // CHUNKS
+        return ref.at[pl.ds(k * size, size)]
+
+    pieces = [(i, k) for k in range(CHUNKS) for i in range(5)]
+    into = [
+        pltpu.make_async_copy(cut(sources[i], k), cut(held[i], k), into_sem.at[i, k])
+        for i, k in pieces
+    ]
+    out = [
+        pltpu.make_async_copy(cut(held[i], k), cut(targets[i], k), out_sem.at[i, k])
+        for i, k in pieces
+    ]
+    for copy in into:
+        copy.start()
+    for first, second in zip(into, out):
+        first.wait()
+        second.start()
+    for copy in out:
+        copy.wait()
+
+
 def per_device(count, *args):
     u, v, t, spin, thick, visc, depth, sea, wet = args
     levels, rows, columns = u.shape
@@ -571,15 +598,14 @@
     vmem = pl.BlockSpec(memory_space=pltpu.VMEM)
     smem = pl.BlockSpec(memory_space=pltpu.SMEM)
     dma = pltpu.SemaphoreType.DMA
-    return pl.pallas_call(
+    fields = pl.pallas_call(
         functools.partial(kernel, count),
         out_shape=[jax.ShapeDtypeStruct(u.shape, f32)] * 3
         + [jax.ShapeDtypeStruct(sea.shape, f32)] * 2,
         in_specs=[anywhere, anywhere, anywhere, vmem, smem, anywhere, anywhere, anywhere, smem],
         out_specs=[anywhere] * 5,
         scratch_shapes=[
-            pltpu.VMEM((3, levels, rows, columns), f32),
-            pltpu.VMEM((4, rows, columns), f32),
+            pltpu.VMEM((rows, columns), f32),
             pltpu.VMEM((2, 3, levels, span, columns), f32),
             pltpu.VMEM((2, 4, span, columns), f32),
             pltpu.VMEM((2, 3, levels, half, columns), f32),
@@ -587,13 +613,11 @@
             pltpu.VMEM((2, 13, span, columns), f32),
             pltpu.VMEM((2, 4, span, columns), f32),
             pltpu.VMEM((peers, 16, columns), f32),
-            dma((3, CHUNKS)),
-            dma((3,)),
-            dma((CHUNKS + 1,)),
-            dma((CHUNKS + 1,)),
-            dma((CHUNKS + 1,)),
-            dma((2, CHUNKS + 1)),
-            dma((2, CHUNKS + 1)),
+            dma((3, CHUNKS + 1)),
+            dma((3, CHUNKS + 1)),
+            dma((3, CHUNKS + 1)),
+            dma((2, 4, CHUNKS + 1)),
+            dma((2, 4, CHUNKS + 1)),
             dma((3, CHUNKS + 1)),
             dma((3, CHUNKS + 1)),
             dma((3, CHUNKS + 1)),
@@ -601,9 +625,18 @@
             dma((peers,)),
         ],
         compiler_params=pltpu.CompilerParams(
-            collective_id=0, has_side_effects=True, vmem_limit_bytes=32 * 1024 * 1024
+            collective_id=0, has_side_effects=True, vmem_limit_bytes=VMEM_BYTES
         ),
-    )(u, v, t, spin.reshape(1, rows), thick, visc, depth, sea, wet)
+    )(u, v, t, spin.reshape(1, rows), thick, visc, depth, sea, wet.T)
+    return pl.pallas_call(
+        deliver,
+        out_shape=[jax.ShapeDtypeStruct(a.shape, f32) for a in fields],
+        in_specs=[anywhere] * 5,
+        out_specs=[anywhere] * 5,
+        scratch_shapes=[pltpu.VMEM(a.shape, f32) for a in fields]
+        + [dma((5, CHUNKS)), dma((5, CHUNKS))],
+        compiler_params=pltpu.CompilerParams(vmem_limit_bytes=VMEM_BYTES),
+    )(*fields)
 
 
 def solution(mesh):

time: 36.3 us -> 29.9 us (0.82)
  local copies, waits for them, and re-layouts: 9.78 us -> 0 us
  Pallas kernels: 25.4 us -> 29 us
    unnamed x22 -> x0, local copies, waits for them, and re-layouts: 9.78 us -> none
    pallas_call x0 -> x1, Pallas kernels: none -> 2.52 us  [per_device(): pl.pallas_call(deliver, out_shape=[jax.ShapeDtypeStruct(a.shape, f32) for...]
    pallas_call x1, Pallas kernels: 25.4 us -> 26.5 us  [per_device(): pl.pallas_call(functools.partial(kernel, count), out_shape=[jax.ShapeDtyp...]
where the time goes in v2:
time: 29.9 us; the launch traced here: 29.7 us
  Pallas kernels  29 us (97%)
  between operations  0.64 us (2%)
    pallas_call x1, Pallas kernels, per_device(): pl.pallas_call(functools.partial(kernel, count), out_shape=[jax.ShapeDtyp...  26.5 us
    pallas_call x1, Pallas kernels, per_device(): pl.pallas_call(deliver, out_shape=[jax.ShapeDtypeStruct(a.shape, f32) for...  2.52 us

profile of v2, /device:TPU:0, one launch (start us, length us, event | category | flops | bytes accessed | tf_op | source)
XLA Modules:
  0.0 29.7 jit_solution(1901203077903289085)
XLA Ops:
  0.6 26.5 %shard_map.128 = (f32[16,64,128]{2,1,0:T(8,128)}, f32[16,64,128]{2,1,0:T(8,128)}, f32[16,64,128]{2,1,0:T(8,128)}, f32[64,128]{1,0:T(8,128)}, f32[64,128]{1,0:T(8,128)}) custom-call(f32[16,64,128]{2,1,0:T(8,128)} %u_ref.1, f32[16,64,128]{2,1,0:T(8,128)} %v_ref.1, f32[16,64,128]{2,1,0:T(8,128)} %t_ref.1, f32[1,64]{1,0:T(1,128)} %bitcast.3, f32[16]{0:T(128)} %thick_ref.1, ...), custom_call_target="tpu_custom_call" | custom-call | tf_op jit(solution)/shard_map/pallas_call | solution.py:601
  27.2 2.5 %shard_map.129 = (f32[16,64,128]{2,1,0:T(8,128)}, f32[16,64,128]{2,1,0:T(8,128)}, f32[16,64,128]{2,1,0:T(8,128)}, f32[64,128]{1,0:T(8,128)}, f32[64,128]{1,0:T(8,128)}) custom-call(f32[16,64,128]{2,1,0:T(8,128)} %get-tuple-element.10.refs_0_, f32[16,64,128]{2,1,0:T(8,128)} %get-tuple-element.11.refs_1_, f32[16,64,128]{2,1,0:T(8,128)} %get-tuple-element.12.refs_2_, ...), custom_call_target="tpu_custom_call" | custom-call | tf_op jit(solution)/shard_map/pallas_call | solution.py:631

commit v3 on v2

--- a/solution.py
+++ b/solution.py
@@ -26,7 +26,7 @@
     count,
     u_ref, v_ref, t_ref, spin_ref, thick_ref, visc_ref, depth_ref, sea_ref, wet_ref,
     ou_ref, ov_ref, ot_ref, ox_ref, or_ref,
-    own_spin, buf, buf2, res, res2, weights, total, gathered,
+    own, own_flat, buf, buf2, res, res2, weights, total, krylov, gathered, own_sem,
     local_sem, swap_send, swap_recv, halo_send, halo_recv,
     out_sem, back_send, back_recv, gram_send, gram_recv,
 ):
@@ -53,12 +53,19 @@
 
     lax.fori_loop(1, peers, greet, 0)
 
+    own_loads = [
+        pltpu.make_async_copy(ref, own.at[f], own_sem.at[f])
+        for f, ref in enumerate((u_ref, v_ref, t_ref))
+    ]
+    for copy in own_loads:
+        copy.start()
+
     spin_row = jnp.broadcast_to(spin_ref[...], (rows, rows))
     diagonal = lax.broadcasted_iota(jnp.int32, (rows, rows), 0) == lax.broadcasted_iota(
         jnp.int32, (rows, rows), 1
     )
     spin_column = jnp.sum(jnp.where(diagonal, spin_row, 0.0), axis=1, keepdims=True)
-    own_spin[...] = jnp.broadcast_to(spin_column, (rows, columns))
+    own_flat[0] = jnp.broadcast_to(spin_column, (rows, columns))
 
     def taken(c):
         return pl.ds(pl.multiple_of((half - HALO) * c, 8), reach)
@@ -68,7 +75,8 @@
 
     has_outer = jnp.where(core == 0, gx > 0, gx < count - 1)
     cells = (u_ref, v_ref, t_ref)
-    flats = (visc_ref, depth_ref, sea_ref, own_spin)
+    flats = (visc_ref, depth_ref, sea_ref) + tuple(own_flat.at[i] for i in range(4))
+    swapped = (0, 1, 2, 4, 5, 6)
 
     def source(f, k, where):
         if k is None:
@@ -131,7 +139,7 @@
         )
 
     def span_of(k):
-        return range(4) if k is None else range(3)
+        return range(7) if k is None else range(3)
 
     def send_halo(k):
         @pl.when(gx < count - 1)
@@ -145,12 +153,13 @@
                 halo_up(f, k).start()
 
     def send_swap(k):
-        for f in range(3):
+        for f in swapped if k is None else range(3):
             swap(f, k).start()
 
     def arrive(k):
         for f in range(3):
             keep(f, k).wait()
+        for f in swapped if k is None else range(3):
             swap(f, k).wait_recv()
 
         @pl.when(has_outer)
@@ -160,7 +169,7 @@
                 halo_in(f, k, 1).wait_recv()
 
     def sent(k):
-        for f in range(3):
+        for f in swapped if k is None else range(3):
             swap(f, k).wait_send()
 
         @pl.when(gx < count - 1)
@@ -177,9 +186,28 @@
     for k in everything:
         for f in range(3):
             keep(f, k).start()
-    own_rows = own_spin[taken(core), :]
+    own_rows = own_flat[0, taken(core), :]
     for h in range(2):
         buf2[h, 3, placed(core), :] = own_rows
+    for copy in own_loads:
+        copy.wait()
+
+    nothing = jnp.zeros((rows, columns), jnp.float32)
+    for i in range(1, 4):
+        own_flat[i] = nothing
+
+    def integrate(l, heat):
+        thickness = thick_ref[l]
+        column = thickness * own[2, l]
+        heat = heat + column
+        own_flat[1] += thickness * own[0, l]
+        own_flat[2] += thickness * own[1, l]
+        own_flat[3] += thickness * (heat - 0.5 * column)
+        return heat
+
+    lax.fori_loop(0, levels, integrate, nothing)
+    for i in range(1, 4):
+        buf2[core, 3 + i, placed(core), :] = own_flat[i, taken(core), :]
     first = gx == 0
     last = gx == count - 1
 
@@ -192,7 +220,7 @@
 
         lax.fori_loop(0, levels, one, 0)
         for h in range(2):
-            for f in range(4):
+            for f in range(7):
                 buf2[h, f, start : start + HALO, :] = jnp.zeros((HALO, columns), jnp.float32)
 
     @pl.when(jnp.logical_and(first, core == 0))
@@ -274,6 +302,135 @@
         for side in range(4):
             weights[h, 8 + side] = viscous[h][side]
         weights[h, 12] = viscous[h][0] + viscous[h][1] + viscous[h][2] + viscous[h][3]
+
+    face = face_weights([buf2[0, 1], buf2[1, 1]])
+    scaling = [
+        surface_coef + (face[h][0] + face[h][1]) + (face[h][2] + face[h][3]) for h in range(2)
+    ]
+    inverse = [1.0 / scaling[h] for h in range(2)]
+    flat = [[buf2[h, f] * mask[h] for h in range(2)] for f in range(4, 7)]
+    rings = [around(pair) for pair in flat]
+    unit = [sides[0][h] + sides[1][h] + sides[2][h] + sides[3][h] for h in range(2)]
+    flow = []
+    for f in range(2):
+        once = [
+            mask[h]
+            * (
+                (rings[f][0][h] + rings[f][1][h])
+                + (rings[f][2][h] + rings[f][3][h])
+                - unit[h] * flat[f][h]
+            )
+            for h in range(2)
+        ]
+        ring = around(once)
+        sign = 1.0 - 2.0 * f
+        total_flow = []
+        for h in range(2):
+            if f == 0:
+                slope = rings[2][1][h] - rings[2][0][h] + weights[h, 6] * flat[2][h]
+            else:
+                slope = rings[2][3][h] - rings[2][2][h] + weights[h, 7] * flat[2][h]
+            smooth = (
+                weights[h, 8] * rings[f][0][h]
+                + weights[h, 9] * rings[f][1][h]
+                + (weights[h, 10] * rings[f][2][h] + weights[h, 11] * rings[f][3][h])
+                - weights[h, 12] * flat[f][h]
+            )
+            twice = (ring[0][h] + ring[1][h]) + (ring[2][h] + ring[3][h]) - unit[h] * once[h]
+            total_flow.append(
+                mask[h]
+                * (
+                    flat[f][h]
+                    + sign * buf2[h, 3] * flat[1 - f][h]
+                    - (0.5 * pressure_coef) * slope
+                    + smooth
+                    - biharmonic_coef * twice
+                )
+            )
+        flow.append(total_flow)
+    flow_u, flow_v = flow
+    before, after = left(flow_v), right(flow_v)
+    vectors = [
+        [
+            mask[h]
+            * (
+                surface_coef * buf2[h, 2]
+                - (0.5 * divergence_coef)
+                * ((down(flow_u[h]) - up(flow_u[h])) + (after[h] - before[h]))
+            )
+            * inverse[h]
+            for h in range(2)
+        ]
+    ]
+    for _ in range(ITERS):
+        ring = around(vectors[-1])
+        vectors.append(
+            [
+                (
+                    (face[h][0] * ring[0][h] + face[h][1] * ring[1][h])
+                    + (face[h][2] * ring[2][h] + face[h][3] * ring[3][h])
+                )
+                * inverse[h]
+                for h in range(2)
+            ]
+        )
+    inside = slice(HALO, HALO + half)
+    basis = [[pair[h][inside] for h in range(2)] for pair in vectors]
+    scale = [scaling[h][inside] for h in range(2)]
+
+    def dot(a, b):
+        both = scale[0] * a[0] * b[0] + scale[1] * a[1] * b[1]
+        return jnp.sum(both, axis=0, keepdims=True)
+
+    moments = 2 * ITERS - 1
+    difference = [
+        [basis[k][h] - basis[k + 1][h] for h in range(2)] for k in range(ITERS)
+    ]
+    gathered[me] = jnp.zeros(gathered.shape[1:], jnp.float32)
+    lines = [dot(basis[(k + 1) // 2], basis[k // 2]) for k in range(moments)]
+    lines += [dot(basis[(k + 1) // 2], difference[k // 2]) for k in range(moments)]
+    for k, line in enumerate(lines):
+        gathered[me, k : k + 1, :] = line
+
+    def gram(k):
+        peer = lax.rem(me + k, peers)
+        return pltpu.make_async_remote_copy(
+            src_ref=gathered.at[me],
+            dst_ref=gathered.at[me],
+            send_sem=gram_send.at[k],
+            recv_sem=gram_recv.at[me],
+            device_id=(group, peer // 2, lax.rem(peer, 2)),
+            device_id_type=MESH,
+        )
+
+    def gram_from(k):
+        peer = lax.rem(me + k, peers)
+        return pltpu.make_async_remote_copy(
+            src_ref=gathered.at[peer],
+            dst_ref=gathered.at[peer],
+            send_sem=gram_send.at[k],
+            recv_sem=gram_recv.at[peer],
+            device_id=(group, peer // 2, lax.rem(peer, 2)),
+            device_id_type=MESH,
+        )
+
+    def gram_start(k, _):
+        gram(k).start()
+        return 0
+
+    def gram_wait(k, _):
+        gram_from(k).wait_recv()
+        return 0
+
+    def gram_sent(k, _):
+        gram(k).wait_send()
+        return 0
+
+    lax.fori_loop(1, peers, gram_start, 0)
+    for h in range(2):
+        for j in range(ITERS + 1):
+            krylov[h, j] = basis[j][h]
+        krylov[h, ITERS + 1] = scale[h]
 
     for h in range(2):
         for i in range(4):
@@ -354,8 +511,6 @@
                 - biharmonic_coef * hyper[1][h]
             )
             t_next = m * (t[h] - (0.25 * advection_coef) * spread + viscous_part[2][h])
-            total[h, 0] += thickness * u_next
-            total[h, 1] += thickness * v_next
             res[h, 0, l] = u_next[HALO : HALO + half]
             res[h, 1, l] = v_next[HALO : HALO + half]
             res[h, 2, l] = t_next[HALO : HALO + half]
@@ -393,91 +548,6 @@
 
     lax.fori_loop(0, CHUNKS, chunk, 0)
 
-    face = face_weights([buf2[0, 1], buf2[1, 1]])
-    scaling = [
-        surface_coef + (face[h][0] + face[h][1]) + (face[h][2] + face[h][3]) for h in range(2)
-    ]
-    inverse = [1.0 / scaling[h] for h in range(2)]
-    flow_u = [total[h, 0] for h in range(2)]
-    flow_v = [total[h, 1] for h in range(2)]
-    before, after = left(flow_v), right(flow_v)
-    vectors = [
-        [
-            mask[h]
-            * (
-                surface_coef * buf2[h, 2]
-                - (0.5 * divergence_coef)
-                * ((down(flow_u[h]) - up(flow_u[h])) + (after[h] - before[h]))
-            )
-            * inverse[h]
-            for h in range(2)
-        ]
-    ]
-    for _ in range(ITERS):
-        ring = around(vectors[-1])
-        vectors.append(
-            [
-                (
-                    (face[h][0] * ring[0][h] + face[h][1] * ring[1][h])
-                    + (face[h][2] * ring[2][h] + face[h][3] * ring[3][h])
-                )
-                * inverse[h]
-                for h in range(2)
-            ]
-        )
-    inside = slice(HALO, HALO + half)
-    basis = [[pair[h][inside] for h in range(2)] for pair in vectors]
-    scale = [scaling[h][inside] for h in range(2)]
-
-    def dot(a, b):
-        both = scale[0] * a[0] * b[0] + scale[1] * a[1] * b[1]
-        return jnp.sum(both, axis=0, keepdims=True)
-
-    moments = 2 * ITERS - 1
-    difference = [
-        [basis[k][h] - basis[k + 1][h] for h in range(2)] for k in range(ITERS)
-    ]
-    gathered[me] = jnp.zeros(gathered.shape[1:], jnp.float32)
-    lines = [dot(basis[(k + 1) // 2], basis[k // 2]) for k in range(moments)]
-    lines += [dot(basis[(k + 1) // 2], difference[k // 2]) for k in range(moments)]
-    for k, line in enumerate(lines):
-        gathered[me, k : k + 1, :] = line
-
-    def gram(k):
-        peer = lax.rem(me + k, peers)
-        return pltpu.make_async_remote_copy(
-            src_ref=gathered.at[me],
-            dst_ref=gathered.at[me],
-            send_sem=gram_send.at[k],
-            recv_sem=gram_recv.at[me],
-            device_id=(group, peer // 2, lax.rem(peer, 2)),
-            device_id_type=MESH,
-        )
-
-    def gram_from(k):
-        peer = lax.rem(me + k, peers)
-        return pltpu.make_async_remote_copy(
-            src_ref=gathered.at[peer],
-            dst_ref=gathered.at[peer],
-            send_sem=gram_send.at[k],
-            recv_sem=gram_recv.at[peer],
-            device_id=(group, peer // 2, lax.rem(peer, 2)),
-            device_id_type=MESH,
-        )
-
-    def gram_start(k, _):
-        gram(k).start()
-        return 0
-
-    def gram_wait(k, _):
-        gram_from(k).wait_recv()
-        return 0
-
-    def gram_sent(k, _):
-        gram(k).wait_send()
-        return 0
-
-    lax.fori_loop(1, peers, gram_start, 0)
     lax.fori_loop(1, peers, gram_wait, 0)
 
     summed = lax.fori_loop(
@@ -520,14 +590,14 @@
             rho = rho_new
 
     for h in range(2):
-        x = guess[0] * basis[0][h]
+        x = guess[0] * krylov[h, 0]
         for j in range(1, ITERS):
-            x = x + guess[j] * basis[j][h]
-        r = remains[0] * basis[0][h]
+            x = x + guess[j] * krylov[h, j]
+        r = remains[0] * krylov[h, 0]
         for j in range(1, ITERS + 1):
-            r = r + remains[j] * basis[j][h]
+            r = r + remains[j] * krylov[h, j]
         res2[h, 0] = x
-        res2[h, 1] = scale[h] * r
+        res2[h, 1] = krylov[h, ITERS + 1] * r
 
     def flat_outs():
         k = CHUNKS
@@ -605,19 +675,22 @@
         in_specs=[anywhere, anywhere, anywhere, vmem, smem, anywhere, anywhere, anywhere, smem],
         out_specs=[anywhere] * 5,
         scratch_shapes=[
-            pltpu.VMEM((rows, columns), f32),
+            pltpu.VMEM((3, levels, rows, columns), f32),
+            pltpu.VMEM((4, rows, columns), f32),
             pltpu.VMEM((2, 3, levels, span, columns), f32),
-            pltpu.VMEM((2, 4, span, columns), f32),
+            pltpu.VMEM((2, 7, span, columns), f32),
             pltpu.VMEM((2, 3, levels, half, columns), f32),
             pltpu.VMEM((2, 2, half, columns), f32),
             pltpu.VMEM((2, 13, span, columns), f32),
             pltpu.VMEM((2, 4, span, columns), f32),
+            pltpu.VMEM((2, ITERS + 2, half, columns), f32),
             pltpu.VMEM((peers, 16, columns), f32),
+            dma((3,)),
             dma((3, CHUNKS + 1)),
-            dma((3, CHUNKS + 1)),
-            dma((3, CHUNKS + 1)),
-            dma((2, 4, CHUNKS + 1)),
-            dma((2, 4, CHUNKS + 1)),
+            dma((7, CHUNKS + 1)),
+            dma((7, CHUNKS + 1)),
+            dma((2, 7, CHUNKS + 1)),
+            dma((2, 7, CHUNKS + 1)),
             dma((3, CHUNKS + 1)),
             dma((3, CHUNKS + 1)),
             dma((3, CHUNKS + 1)),

time: 29.9 us -> 27.1 us (0.906)
  the two profiles are of different devices: /device:TPU:0 before, /device:TPU:5 now
where the time goes in v3:
time: 27.1 us; the launch traced here: 26.9 us
  Pallas kernels  26.2 us (97%)
  between operations  0.64 us (2%)
    pallas_call x1, Pallas kernels, per_device(): pl.pallas_call(functools.partial(kernel, count), out_shape=[jax.ShapeDtyp...  23.7 us
    pallas_call x1, Pallas kernels, per_device(): pl.pallas_call(deliver, out_shape=[jax.ShapeDtypeStruct(a.shape, f32) for...  2.52 us

profile of v3, /device:TPU:5, one launch (start us, length us, event | category | flops | bytes accessed | tf_op | source)
XLA Modules:
  0.0 26.9 jit_solution(9934286442919887253)
XLA Ops:
  0.6 23.7 %shard_map.128 = (f32[16,64,128]{2,1,0:T(8,128)}, f32[16,64,128]{2,1,0:T(8,128)}, f32[16,64,128]{2,1,0:T(8,128)}, f32[64,128]{1,0:T(8,128)}, f32[64,128]{1,0:T(8,128)}) custom-call(f32[16,64,128]{2,1,0:T(8,128)} %u_ref.1, f32[16,64,128]{2,1,0:T(8,128)} %v_ref.1, f32[16,64,128]{2,1,0:T(8,128)} %t_ref.1, f32[1,64]{1,0:T(1,128)} %bitcast.3, f32[16]{0:T(128)} %thick_ref.1, ...), custom_call_target="tpu_custom_call" | custom-call | tf_op jit(solution)/shard_map/pallas_call | solution.py:671
  24.3 2.5 %shard_map.129 = (f32[16,64,128]{2,1,0:T(8,128)}, f32[16,64,128]{2,1,0:T(8,128)}, f32[16,64,128]{2,1,0:T(8,128)}, f32[64,128]{1,0:T(8,128)}, f32[64,128]{1,0:T(8,128)}) custom-call(f32[16,64,128]{2,1,0:T(8,128)} %get-tuple-element.10.refs_0_, f32[16,64,128]{2,1,0:T(8,128)} %get-tuple-element.11.refs_1_, f32[16,64,128]{2,1,0:T(8,128)} %get-tuple-element.12.refs_2_, ...), custom_call_target="tpu_custom_call" | custom-call | tf_op jit(solution)/shard_map/pallas_call | solution.py:704

commit v4 on v3

--- a/solution.py
+++ b/solution.py
@@ -11,6 +11,7 @@
 ITERS = 3
 CHUNKS = 4
 HALO = 8
+NEAR = 2
 VMEM_BYTES = 60 * 1024 * 1024
 
 pressure_coef = 0.02
@@ -108,10 +109,13 @@
             local_sem.at[f, slot(k)],
         )
 
+    def depth_of(k):
+        return HALO if k is None else NEAR
+
     def halo_down(f, k):
         return pltpu.make_async_remote_copy(
-            src_ref=source(f, k, pl.ds(rows - HALO, HALO)),
-            dst_ref=target(f, k, core, pl.ds(0, HALO)),
+            src_ref=source(f, k, pl.ds(rows - depth_of(k), depth_of(k))),
+            dst_ref=target(f, k, core, pl.ds(HALO - depth_of(k), depth_of(k))),
             send_sem=halo_send.at[0, f, slot(k)],
             recv_sem=halo_recv.at[core, f, slot(k)],
             device_id=(group, lax.rem(gx + 1, count), 0),
@@ -120,8 +124,8 @@
 
     def halo_up(f, k):
         return pltpu.make_async_remote_copy(
-            src_ref=source(f, k, pl.ds(0, HALO)),
-            dst_ref=target(f, k, core, pl.ds(HALO + half, HALO)),
+            src_ref=source(f, k, pl.ds(0, depth_of(k))),
+            dst_ref=target(f, k, core, pl.ds(HALO + half, depth_of(k))),
             send_sem=halo_send.at[1, f, slot(k)],
             recv_sem=halo_recv.at[core, f, slot(k)],
             device_id=(group, lax.rem(gx + count - 1, count), 1),
@@ -130,8 +134,8 @@
 
     def halo_in(f, k, h):
         return pltpu.make_async_remote_copy(
-            src_ref=source(f, k, pl.ds(0, HALO)),
-            dst_ref=target(f, k, h, pl.ds(0, HALO)),
+            src_ref=source(f, k, pl.ds(0, depth_of(k))),
+            dst_ref=target(f, k, h, pl.ds(HALO - depth_of(k), depth_of(k))),
             send_sem=halo_send.at[0, f, slot(k)],
             recv_sem=halo_recv.at[h, f, slot(k)],
             device_id=(group, gx, other),

time: 27.1 us -> 22.8 us (0.84)
  the two profiles are of different devices: /device:TPU:5 before, /device:TPU:0 now
where the time goes in v4:
time: 22.8 us; the launch traced here: 22.6 us
  Pallas kernels  22 us (96%)
  between operations  0.64 us (3%)
    pallas_call x1, Pallas kernels, per_device(): pl.pallas_call(functools.partial(kernel, count), out_shape=[jax.ShapeDtyp...  19.5 us
    pallas_call x1, Pallas kernels, per_device(): pl.pallas_call(deliver, out_shape=[jax.ShapeDtypeStruct(a.shape, f32) for...  2.52 us

profile of v4, /device:TPU:0, one launch (start us, length us, event | category | flops | bytes accessed | tf_op | source)
XLA Modules:
  0.0 22.6 jit_solution(5397994238978676889)
XLA Ops:
  0.6 19.5 %shard_map.128 = (f32[16,64,128]{2,1,0:T(8,128)}, f32[16,64,128]{2,1,0:T(8,128)}, f32[16,64,128]{2,1,0:T(8,128)}, f32[64,128]{1,0:T(8,128)}, f32[64,128]{1,0:T(8,128)}) custom-call(f32[16,64,128]{2,1,0:T(8,128)} %u_ref.1, f32[16,64,128]{2,1,0:T(8,128)} %v_ref.1, f32[16,64,128]{2,1,0:T(8,128)} %t_ref.1, f32[1,64]{1,0:T(1,128)} %bitcast.3, f32[16]{0:T(128)} %thick_ref.1, ...), custom_call_target="tpu_custom_call" | custom-call | tf_op jit(solution)/shard_map/pallas_call | solution.py:675
  20.1 2.5 %shard_map.129 = (f32[16,64,128]{2,1,0:T(8,128)}, f32[16,64,128]{2,1,0:T(8,128)}, f32[16,64,128]{2,1,0:T(8,128)}, f32[64,128]{1,0:T(8,128)}, f32[64,128]{1,0:T(8,128)}) custom-call(f32[16,64,128]{2,1,0:T(8,128)} %get-tuple-element.10.refs_0_, f32[16,64,128]{2,1,0:T(8,128)} %get-tuple-element.11.refs_1_, f32[16,64,128]{2,1,0:T(8,128)} %get-tuple-element.12.refs_2_, ...), custom_call_target="tpu_custom_call" | custom-call | tf_op jit(solution)/shard_map/pallas_call | solution.py:708
